TPU v7x, 32 devices: a whole 2x2x4 slice. The times are simulated.
32 devices in a mesh: rows: 32 (over z, y, x, core).
Axes of the slice: x: 2, y: 2, z: 4, core: 2. Of those that a mesh axis runs over, the one named last changes fastest.
Arguments:
- points_t: float32 [64, 32768], P(None, 'rows'), may hold values from -6 to 6
- pivots: int32 [2, 256], replicated, may hold values from 0 to 32767, as said below
Outputs:
- factor: bfloat16 [32768, 512], P('rows')
- residual_diag: float32 [32768], P('rows')
Inputs may be any that keep to these rules, and one draw needn't show every extreme that they name: `pivots`: all 512 indices are different. In each block at most 10 indices fall in one device's points, rows k * 1024 to (k + 1) * 1024 - 1, and in each block some device holds exactly 10.
All inputs are finite; a program needn't handle non-finite values.
Results may differ from a plain program's by a relative error of at most 0.001.
Values sent between devices are 32-bit elements; how exact they have to be, the bound alone decides.
No kernel may reach another device: no remote copies, remote signals or barrier semaphores. Data moves between devices by JAX's collectives and lax.ppermute only.
A program may use at most 64 MiB of HBM per device.

v0:
```python
import functools

import jax
import jax.numpy as jnp
from jax import lax
from jax.experimental import pallas as pl
from jax.experimental.pallas import tpu as pltpu
from jax.sharding import PartitionSpec as P

PANEL = 128
STEP = 8
LANES = 128


def halves(x):
    high = x.astype(jnp.bfloat16)
    return high, (x - high.astype(jnp.float32)).astype(jnp.bfloat16)


def thirds(x):
    high = x.astype(jnp.bfloat16)
    rest = x - high.astype(jnp.float32)
    mid, low = halves(rest)
    return high, mid, low


def nt_dot(left, right):
    return lax.dot_general(
        left, right, (((1,), (1,)), ((), ())), preferred_element_type=jnp.float32
    )


def left_form(x):
    high, low = halves(x)
    return jnp.concatenate([high, high, low], axis=1)


def right_form(x):
    high, low = halves(x)
    return jnp.concatenate([high, low, high], axis=1)


def exponent_operands(x, left, right):
    rows = x.shape[0]
    half = [-h for h in thirds(0.5 * jnp.sum(x * x, axis=1, keepdims=True))]
    one = jnp.ones((rows, 3), jnp.bfloat16)
    pad = jnp.zeros((rows, 256 - 3 * x.shape[1] - 6), jnp.bfloat16)
    high, low = halves(x)
    result = []
    if left:
        result.append(jnp.concatenate([high, high, low] + half + [one, pad], axis=1))
    if right:
        result.append(jnp.concatenate([high, low, high, one] + half + [pad], axis=1))
    return result


def lane_spread(x, lane):
    return jnp.broadcast_to(x[:, lane : lane + 1], (STEP, LANES))


def row_spread(x, row):
    return jnp.broadcast_to(x[row : row + 1, :], (STEP, LANES))


def panel_inverse(tiles):
    lane = lax.broadcasted_iota(jnp.int32, (STEP, LANES), 1)
    sub = lax.broadcasted_iota(jnp.int32, (STEP, LANES), 0)
    tiles = list(tiles)
    result = []
    for s in range(len(tiles)):
        first = STEP * s
        inside = (lane >= first) & (lane < first + STEP)
        cols = [lane_spread(tiles[s], first + k) for k in range(STEP)]
        e = {(i, k): row_spread(cols[k], i) for k in range(STEP) for i in range(k, STEP)}
        low = {}
        inv = []
        for k in range(STEP):
            inv.append(lax.rsqrt(e[k, k]))
            for i in range(k + 1, STEP):
                low[i, k] = e[i, k] * inv[k]
            for m in range(k + 1, STEP):
                for i in range(m, STEP):
                    e[i, m] = e[i, m] - low[i, k] * low[m, k]
        own = jnp.where(inside, jnp.where(lane - first == sub, 1.0, 0.0), tiles[s])
        upper = []
        for i in range(STEP):
            acc = row_spread(own, i)
            for m in range(i):
                acc = acc - low[i, m] * upper[m]
            upper.append(acc * inv[i])
        done = upper[0]
        for i in range(1, STEP):
            done = jnp.where(sub == i, upper[i], done)
        result.append(jnp.where(lane < first + STEP, done, 0.0))
        full = None
        for t in range(s + 1, len(tiles)):
            cols = [lane_spread(tiles[t], first + k) for k in range(STEP)]
            acc = jnp.where(inside, 0.0, tiles[t])
            if t == s + 1:
                mine = []
                for k in range(STEP):
                    col = cols[k]
                    for m in range(k):
                        col = col - low[k, m] * mine[m]
                    mine.append(col * inv[k])
                    acc = acc - mine[k] * upper[k]
            else:
                if full is None:
                    full = [None] * STEP
                    for i in reversed(range(STEP)):
                        back = upper[i]
                        for m in range(i + 1, STEP):
                            back = back - low[m, i] * full[m]
                        full[i] = back * inv[i]
                for k in range(STEP):
                    acc = acc - cols[k] * full[k]
            tiles[t] = acc
    return result


def factor_kernel(points_ref, pivots_ref, factor_ref, diag_ref, work, squares):
    rows = factor_ref.shape[0]
    width = factor_ref.shape[1]
    scale = (2.0 / (1.65 * pivots_ref.shape[1])) ** 0.5
    piv_left, piv_right = exponent_operands(pivots_ref[...] * scale, True, True)
    work[:width, :] = jnp.exp(nt_dot(piv_left, piv_right))
    work[width:, :] = jnp.exp(nt_dot(points_ref[...], piv_right))
    for first in range(0, width, PANEL):
        last = first + PANEL
        inverse = jnp.concatenate(
            panel_inverse(
                [work[first + r : first + r + STEP, first:last] for r in range(0, PANEL, STEP)]
            ),
            axis=0,
        )
        new = nt_dot(left_form(work[last:, first:last]), right_form(inverse))
        if last < width:
            below = new[: width - last]
            work[last:, last:] = work[last:, last:] - nt_dot(left_form(new), right_form(below))
        mine = new[width - last :]
        factor_ref[:, first:last] = mine.astype(jnp.bfloat16)
        squares[...] = mine * mine if first == 0 else squares[...] + mine * mine
    ones = jnp.ones((STEP, 3 * PANEL), jnp.bfloat16)
    sums = nt_dot(ones, jnp.concatenate(thirds(squares[...]), axis=1))
    diag_ref[...] = 1.0 - sums[:1]


def prepare_kernel(points_ref, out_ref):
    scale = (2.0 / (1.65 * points_ref.shape[0])) ** 0.5
    out_ref[...] = exponent_operands(points_ref[...].T * scale, True, False)[0]


VMEM = pl.BlockSpec(memory_space=pltpu.VMEM)


def prepare(points_t):
    return pl.pallas_call(
        prepare_kernel,
        out_shape=jax.ShapeDtypeStruct((points_t.shape[1], 256), jnp.bfloat16),
        in_specs=[VMEM],
        out_specs=VMEM,
        compiler_params=pltpu.CompilerParams(vmem_limit_bytes=32 * 2**20),
    )(points_t)


def factorize(points, pivot_pts):
    rows, width = points.shape[0], pivot_pts.shape[0]
    return pl.pallas_call(
        factor_kernel,
        out_shape=[
            jax.ShapeDtypeStruct((rows, width), jnp.bfloat16),
            jax.ShapeDtypeStruct((1, rows), jnp.float32),
        ],
        in_specs=[VMEM, VMEM],
        out_specs=[VMEM, VMEM],
        scratch_shapes=[
            pltpu.VMEM((width + rows, width), jnp.float32),
            pltpu.VMEM((rows, PANEL), jnp.float32),
        ],
        compiler_params=pltpu.CompilerParams(vmem_limit_bytes=48 * 2**20),
    )(points, pivot_pts)


def digits_of(ndev):
    rounds = []
    left = ndev
    while left > 1:
        radix = 4 if left % 8 == 0 else 2
        left //= radix
        rounds.append((radix, left))
    return rounds


def gather_relative(buffer, ndev):
    held = buffer[None]
    for radix, stride in digits_of(ndev):
        pieces = [held]
        for step in range(1, radix):
            pairs = []
            for d in range(ndev):
                digit = (d // stride) % radix
                pairs.append((d, d + ((digit + step) % radix - digit) * stride))
            pieces.append(lax.ppermute(held, "rows", pairs))
        held = jnp.concatenate(pieces, axis=0)
    return held


def place_of(owner, me, ndev):
    place = jnp.zeros_like(owner)
    scale = 1
    for radix, stride in digits_of(ndev):
        rel = (me // stride % radix - owner // stride % radix + radix) % radix
        place = place + rel * scale
        scale *= radix
    return place


def body(points_t, pivots):
    ndev = lax.axis_size("rows")
    dim, rows_here = points_t.shape
    blocks, piv = pivots.shape
    me = lax.axis_index("rows")
    capacity = piv // ndev + 2
    owner = pivots // rows_here
    earlier = lax.broadcasted_iota(jnp.int32, (piv, piv), 0) > lax.broadcasted_iota(
        jnp.int32, (piv, piv), 1
    )
    same = (owner[:, :, None] == owner[:, None, :]) & earlier[None]
    slot = jnp.sum(jnp.where(same, 1, 0), axis=2).astype(jnp.int32)
    slot_ids = lax.broadcasted_iota(jnp.int32, (blocks, capacity, piv), 1)
    hit = (slot_ids == slot[:, None, :]) & (owner[:, None, :] == me)
    column = jnp.sum(jnp.where(hit, (pivots - me * rows_here)[:, None, :] + 1, 0), axis=2) - 1
    col_ids = lax.broadcasted_iota(jnp.int32, (blocks, capacity, rows_here), 2)
    pick = jnp.where(col_ids == column[:, :, None], 1.0, 0.0).astype(jnp.float32)
    picked = lax.dot_general(
        pick.reshape(blocks * capacity, rows_here),
        points_t,
        (((1,), (1,)), ((), ())),
        precision=lax.Precision.HIGHEST,
        preferred_element_type=jnp.float32,
    ).reshape(blocks, capacity, dim)
    buffer = jnp.concatenate([picked[b] for b in range(blocks)], axis=1)
    gathered = gather_relative(buffer, ndev).reshape(ndev * capacity, blocks * dim)
    target = place_of(owner, me, ndev) * capacity + slot
    place_ids = lax.broadcasted_iota(jnp.int32, (blocks, ndev * capacity, piv), 1)
    placer = jnp.where(place_ids == target[:, None, :], 1.0, 0.0).astype(jnp.float32)
    pivot_pts = jnp.concatenate(
        [
            lax.dot_general(
                placer[b],
                gathered[:, b * dim : (b + 1) * dim],
                (((0,), (0,)), ((), ())),
                precision=lax.Precision.HIGHEST,
                preferred_element_type=jnp.float32,
            )
            for b in range(blocks)
        ],
        axis=0,
    )
    factor, diag = factorize(prepare(points_t), pivot_pts)
    return (factor, diag.reshape(rows_here))


def solution(mesh):
    return jax.shard_map(
        body,
        mesh=mesh,
        in_specs=(P(None, "rows"), P()),
        out_specs=(P("rows", None), P("rows")),
        check_vma=False,
    )
```

profile of v0, /device:TPU:0, one launch (start us, length us, event | category | flops | bytes accessed | tf_op | source)
XLA Modules:
  0.0 46.7 jit_solution(14613475422720687180)
XLA Ops:
  0.7 0.0 copy-start.1
  0.7 0.7 %copy-done.1 = s32[2,256]{1,0:T(2,128)S(1)} copy-done((s32[2,256]{1,0:T(2,128)S(1)}, s32[2,256]{1,0:T(2,128)}, u32[]{:S(2)}) %copy-start.1) | copy-done | bytes 2072
  1.4 0.3 select_reduce_fusion
  1.7 0.3 fusion.10
  1.9 0.1 copy.16
  2.0 0.1 sub.67
  2.1 1.3 %fusion.5 = f32[20,64]{1,0:T(8,128)S(1)} fusion(f32[64,1024]{1,0:T(8,128)} %points_ref.1, s32[20]{0:T(128)S(1)} %sub.67), kind=kOutput, calls=%fused_computation.11 | convolution fusion | flops 15769600 | bytes 267344 | tf_op jit(solution)/shard_map/dot_general | solution.py:235
  3.4 0.1 fusion.27
  3.4 0.1 constant_dynamic-update-slice_fusion.6
  3.5 5.1 %collective-permute-start.2 = (f32[1,10,128]{2,1,0:T(8,128)S(1)}, f32[1,10,128]{2,1,0:T(8,128)S(1)}, u32[]{:S(2)}, u32[]{:S(2)}) collective-permute-start(f32[1,10,128]{2,1,0:T(8,128)S(1)} %get-tuple-element.7), channel_id=1, source_target_pairs={{0,24},{1,25},{2,26},{3,27},{4,28},{5,29},{6,30},{7,31},{8,0},{9,1... | collective-permute-start | bytes 15368 | tf_op jit(solution)/shard_map/ppermute | solution.py:203
  8.6 0.0 collective-permute-start.1
  8.6 1.0 %collective-permute-start = (f32[1,10,128]{2,1,0:T(8,128)S(1)}, f32[1,10,128]{2,1,0:T(8,128)S(1)}, u32[]{:S(2)}, u32[]{:S(2)}) collective-permute-start(f32[1,10,128]{2,1,0:T(8,128)S(1)} %get-tuple-element.7), channel_id=1, source_target_pairs={{0,8},{1,9},{2,10},{3,11},{4,12},{5,13},{6,14},{7,15},{8,16},{9,17... | collective-permute-start | bytes 15368 | tf_op jit(solution)/shard_map/ppermute | solution.py:203
  9.6 0.3 collective-permute-done.2
  9.9 3.2 %collective-permute-done.1 = f32[1,10,128]{2,1,0:T(8,128)S(1)} collective-permute-done((f32[1,10,128]{2,1,0:T(8,128)S(1)}, f32[1,10,128]{2,1,0:T(8,128)S(1)}, u32[]{:S(2)}, u32[]{:S(2)}) %collective-permute-start.1) | collective-permute-done | bytes 5152 | tf_op jit(solution)/shard_map/ppermute | solution.py:203
  13.1 0.9 %collective-permute-done = f32[1,10,128]{2,1,0:T(8,128)S(1)} collective-permute-done((f32[1,10,128]{2,1,0:T(8,128)S(1)}, f32[1,10,128]{2,1,0:T(8,128)S(1)}, u32[]{:S(2)}, u32[]{:S(2)}) %collective-permute-start) | collective-permute-done | bytes 5152 | tf_op jit(solution)/shard_map/ppermute | solution.py:203
  14.0 2.4 %collective-permute-start.5 = (f32[4,10,128]{2,1,0:T(8,128)S(1)}, f32[4,10,128]{2,1,0:T(8,128)S(1)}, u32[]{:S(2)}, u32[]{:S(2)}) collective-permute-start(f32[4,10,128]{2,1,0:T(8,128)S(1)} %pad_maximum_fusion.1), channel_id=1, source_target_pairs={{0,6},{1,7},{2,0},{3,1},{4,2},{5,3},{6,4},{7,5},{8,14},{9,15},{10,... | collective-permute-start | bytes 61448 | tf_op jit(solution)/shard_map/ppermute | solution.py:203
  16.5 0.5 %collective-permute-start.4 = (f32[4,10,128]{2,1,0:T(8,128)S(1)}, f32[4,10,128]{2,1,0:T(8,128)S(1)}, u32[]{:S(2)}, u32[]{:S(2)}) collective-permute-start(f32[4,10,128]{2,1,0:T(8,128)S(1)} %pad_maximum_fusion.1), channel_id=1, source_target_pairs={{0,4},{1,5},{2,6},{3,7},{4,0},{5,1},{6,2},{7,3},{8,12},{9,13},{10,... | collective-permute-start | bytes 61448 | tf_op jit(solution)/shard_map/ppermute | solution.py:203
  17.0 0.6 %collective-permute-start.3 = (f32[4,10,128]{2,1,0:T(8,128)S(1)}, f32[4,10,128]{2,1,0:T(8,128)S(1)}, u32[]{:S(2)}, u32[]{:S(2)}) collective-permute-start(f32[4,10,128]{2,1,0:T(8,128)S(1)} %pad_maximum_fusion.1), channel_id=1, source_target_pairs={{0,2},{1,3},{2,4},{3,5},{4,6},{5,7},{6,0},{7,1},{8,10},{9,11},{10,... | collective-permute-start | bytes 61448 | tf_op jit(solution)/shard_map/ppermute | solution.py:203
  17.6 4.2 %collective-permute-done.3 = f32[4,10,128]{2,1,0:T(8,128)S(1)} collective-permute-done((f32[4,10,128]{2,1,0:T(8,128)S(1)}, f32[4,10,128]{2,1,0:T(8,128)S(1)}, u32[]{:S(2)}, u32[]{:S(2)}) %collective-permute-start.3) | collective-permute-done | bytes 20512 | tf_op jit(solution)/shard_map/ppermute | solution.py:203
  21.8 0.0 collective-permute-done.4
  21.8 0.0 collective-permute-done.5
  21.8 0.0 copy-start
  21.9 0.1 collective-permute-start.6
  21.9 0.1 fusion
  22.0 0.8 %copy-done = f32[64,1024]{1,0:T(8,128)S(1)} copy-done((f32[64,1024]{1,0:T(8,128)S(1)}, f32[64,1024]{1,0:T(8,128)}, u32[]{:S(2)}) %copy-start) | copy-done | bytes 262168
  22.8 0.5 shard_map.41.points_ref
  23.3 0.0 collective-permute-done.6
  23.3 0.9 %fusion.1 = f32[256,64]{1,0:T(8,128)S(1)} fusion(f32[2,320,256]{2,1,0:T(8,128)S(1)} %fusion, f32[320,128]{1,0:T(8,128)S(1)} %reshape.40), kind=kOutput, calls=%fused_computation.4 | convolution fusion | flops 62914560 | bytes 557056 | tf_op jit(solution)/shard_map/dot_general | solution.py:249
  24.2 0.8 %fusion.2 = f32[256,64]{1,0:T(8,128)S(1)} fusion(f32[2,320,256]{2,1,0:T(8,128)S(1)} %fusion, f32[320,128]{1,0:T(8,128)S(1)} %reshape.40), kind=kOutput, calls=%fused_computation.6 | convolution fusion | flops 62914560 | bytes 557056 | tf_op jit(solution)/shard_map/dot_general | solution.py:249
  25.0 21.7 %shard_map.42 = (bf16[1024,512]{1,0:T(8,128)(2,1)}, f32[1,1024]{1,0:T(1,128)}) custom-call(bf16[1024,256]{1,0:T(8,128)(2,1)S(1)} %shard_map.41.points_ref, f32[512,64]{1,0:T(8,128)S(1)} %pad_maximum_fusion.pivots_ref), custom_call_target="tpu_custom_call" | custom-call | tf_op jit(solution)/shard_map/pallas_call | solution.py:168
  (16 shorter events, 0.2 us)
Async XLA Ops:
  0.7 0.7 %copy-start.1 = (s32[2,256]{1,0:T(2,128)S(1)}, s32[2,256]{1,0:T(2,128)}, u32[]{:S(2)}) copy-start(s32[2,256]{1,0:T(2,128)} %param.3) | copy-start | bytes 6148
  3.5 6.4 %collective-permute-start.2 = (f32[1,10,128]{2,1,0:T(8,128)S(1)}, f32[1,10,128]{2,1,0:T(8,128)S(1)}, u32[]{:S(2)}, u32[]{:S(2)}) collective-permute-start(f32[1,10,128]{2,1,0:T(8,128)S(1)} %get-tuple-element.7), channel_id=1, source_target_pairs={{0,24},{1,25},{2,26},{3,27},{4,28},{5,29},{6,30},{7,31},{8,0},{9,1... | collective-permute-start | bytes 15368 | tf_op jit(solution)/shard_map/ppermute | solution.py:203
  8.6 4.5 %collective-permute-start.1 = (f32[1,10,128]{2,1,0:T(8,128)S(1)}, f32[1,10,128]{2,1,0:T(8,128)S(1)}, u32[]{:S(2)}, u32[]{:S(2)}) collective-permute-start(f32[1,10,128]{2,1,0:T(8,128)S(1)} %get-tuple-element.7), channel_id=1, source_target_pairs={{0,16},{1,17},{2,18},{3,19},{4,20},{5,21},{6,22},{7,23},{8,24},{9,... | collective-permute-start | bytes 15368 | tf_op jit(solution)/shard_map/ppermute | solution.py:203
  8.6 5.4 %collective-permute-start = (f32[1,10,128]{2,1,0:T(8,128)S(1)}, f32[1,10,128]{2,1,0:T(8,128)S(1)}, u32[]{:S(2)}, u32[]{:S(2)}) collective-permute-start(f32[1,10,128]{2,1,0:T(8,128)S(1)} %get-tuple-element.7), channel_id=1, source_target_pairs={{0,8},{1,9},{2,10},{3,11},{4,12},{5,13},{6,14},{7,15},{8,16},{9,17... | collective-permute-start | bytes 15368 | tf_op jit(solution)/shard_map/ppermute | solution.py:203
  14.0 7.8 %collective-permute-start.5 = (f32[4,10,128]{2,1,0:T(8,128)S(1)}, f32[4,10,128]{2,1,0:T(8,128)S(1)}, u32[]{:S(2)}, u32[]{:S(2)}) collective-permute-start(f32[4,10,128]{2,1,0:T(8,128)S(1)} %pad_maximum_fusion.1), channel_id=1, source_target_pairs={{0,6},{1,7},{2,0},{3,1},{4,2},{5,3},{6,4},{7,5},{8,14},{9,15},{10,... | collective-permute-start | bytes 61448 | tf_op jit(solution)/shard_map/ppermute | solution.py:203
  16.5 5.3 %collective-permute-start.4 = (f32[4,10,128]{2,1,0:T(8,128)S(1)}, f32[4,10,128]{2,1,0:T(8,128)S(1)}, u32[]{:S(2)}, u32[]{:S(2)}) collective-permute-start(f32[4,10,128]{2,1,0:T(8,128)S(1)} %pad_maximum_fusion.1), channel_id=1, source_target_pairs={{0,4},{1,5},{2,6},{3,7},{4,0},{5,1},{6,2},{7,3},{8,12},{9,13},{10,... | collective-permute-start | bytes 61448 | tf_op jit(solution)/shard_map/ppermute | solution.py:203
  17.0 4.8 %collective-permute-start.3 = (f32[4,10,128]{2,1,0:T(8,128)S(1)}, f32[4,10,128]{2,1,0:T(8,128)S(1)}, u32[]{:S(2)}, u32[]{:S(2)}) collective-permute-start(f32[4,10,128]{2,1,0:T(8,128)S(1)} %pad_maximum_fusion.1), channel_id=1, source_target_pairs={{0,2},{1,3},{2,4},{3,5},{4,6},{5,7},{6,0},{7,1},{8,10},{9,11},{10,... | collective-permute-start | bytes 61448 | tf_op jit(solution)/shard_map/ppermute | solution.py:203
  21.8 1.0 %copy-start = (f32[64,1024]{1,0:T(8,128)S(1)}, f32[64,1024]{1,0:T(8,128)}, u32[]{:S(2)}) copy-start(f32[64,1024]{1,0:T(8,128)} %points_ref.1) | copy-start | bytes 786436
  21.9 1.4 %collective-permute-start.6 = (f32[16,10,128]{2,1,0:T(8,128)S(1)}, f32[16,10,128]{2,1,0:T(8,128)S(1)}, u32[]{:S(2)}, u32[]{:S(2)}) collective-permute-start(f32[16,10,128]{2,1,0:T(8,128)S(1)} %get-tuple-element.10), channel_id=1, source_target_pairs={{0,1},{1,0},{2,3},{3,2},{4,5},{5,4},{6,7},{7,6},{8,9},{9,8},{10,11... | collective-permute-start | bytes 245768 | tf_op jit(solution)/shard_map/ppermute | solution.py:203
where the time goes:
time: 46.9 us; the launch traced here: 46.7 us
  Pallas kernels  22.1 us (47%)
  starting transfers between devices  9.68 us (21%)
  waiting for transfers between devices  8.61 us (18%)
  matrix products  2.95 us (6%)
  local copies, waits for them, and re-layouts  1.77 us (4%)
  between operations  0.8 us (2%)
  other arithmetic  0.77 us (2%)
    pallas_call x1, Pallas kernels, factorize(): pl.pallas_call(factor_kernel, out_shape=[jax.ShapeDtypeStruct((rows, widt...  21.7 us
    ppermute x7, starting transfers between devices, gather_relative(): pieces.append(lax.ppermute(held, 'rows', pairs))  9.68 us
    ppermute x7, waiting for transfers between devices, gather_relative(): pieces.append(lax.ppermute(held, 'rows', pairs))  8.61 us
    dot_general x2, matrix products, body(): lax.dot_general(placer[b], gathered[:, b * dim:(b + 1) * dim], (((0,), (0...  1.67 us
    unnamed x11, local copies, waits for them, and re-layouts  1.6 us
    dot_general x1, matrix products, body(): lax.dot_general(pick.reshape(blocks * capacity, rows_here), points_t, (((...  1.28 us
  transfers between devices with their start and end apart: 7, of which 4 were waited for; matrix products, arithmetic and copies ran while one was open for 0% of the time, Pallas kernels for 1%

commit v1 on v0

v1 whole, which is shorter than its diff:
```python
import functools

import jax
import jax.numpy as jnp
from jax import lax
from jax.experimental import pallas as pl
from jax.experimental.pallas import tpu as pltpu
from jax.sharding import PartitionSpec as P

PANEL = 128
STEP = 8
LANES = 128
CHUNK = 128


def halves(x):
    high = x.astype(jnp.bfloat16)
    return high, (x - high.astype(jnp.float32)).astype(jnp.bfloat16)


def thirds(x):
    high = x.astype(jnp.bfloat16)
    mid, low = halves(x - high.astype(jnp.float32))
    return high, mid, low


def nn_dot(left, right):
    return jnp.dot(left, right, preferred_element_type=jnp.float32)


def nt_dot(left, right):
    return lax.dot_general(
        left, right, (((1,), (1,)), ((), ())), preferred_element_type=jnp.float32
    )


def left_form(x):
    high, low = halves(x)
    return jnp.concatenate([high, high, low], axis=1)


def right_form(x):
    high, low = halves(x)
    return jnp.concatenate([high, low, high], axis=1)


def exponent_operands(x, left, right):
    rows = x.shape[0]
    half = [-h for h in thirds(0.5 * jnp.sum(x * x, axis=1, keepdims=True))]
    one = jnp.ones((rows, 3), jnp.bfloat16)
    pad = jnp.zeros((rows, 256 - 3 * x.shape[1] - 6), jnp.bfloat16)
    high, low = halves(x)
    result = []
    if left:
        result.append(jnp.concatenate([high, high, low] + half + [one, pad], axis=1))
    if right:
        result.append(jnp.concatenate([high, low, high, one] + half + [pad], axis=1))
    return result


def lane_spread(x, lane):
    return jnp.broadcast_to(x[:, lane : lane + 1], (STEP, LANES))


def row_spread(x, row):
    return jnp.broadcast_to(x[row : row + 1, :], (STEP, LANES))


def small_factor(e):
    low = {}
    inv = {}
    for k in range(0, STEP, 2):
        det = e[k, k] * e[k + 1, k + 1] - e[k + 1, k] * e[k + 1, k]
        inv[k] = lax.rsqrt(e[k, k])
        inv[k + 1] = e[k, k] * lax.rsqrt(e[k, k] * det)
        low[k + 1, k] = e[k + 1, k] * inv[k]
        for i in range(k + 2, STEP):
            low[i, k] = e[i, k] * inv[k]
            low[i, k + 1] = (e[i, k + 1] - low[i, k] * low[k + 1, k]) * inv[k + 1]
        for m in range(k + 2, STEP):
            for i in range(m, STEP):
                e[i, m] = e[i, m] - low[i, k] * low[m, k] - low[i, k + 1] * low[m, k + 1]
    return low, inv


def panel_inverse(tiles, jobs):
    lane = lax.broadcasted_iota(jnp.int32, (STEP, LANES), 1)
    sub = lax.broadcasted_iota(jnp.int32, (STEP, LANES), 0)
    tiles = list(tiles)
    jobs = list(jobs)
    result = []
    for s in range(len(tiles)):
        first = STEP * s
        inside = (lane >= first) & (lane < first + STEP)
        cols = [lane_spread(tiles[s], first + k) for k in range(STEP)]
        e = {(i, k): row_spread(cols[k], i) for k in range(STEP) for i in range(k, STEP)}
        low, inv = small_factor(e)
        own = jnp.where(inside, jnp.where(lane - first == sub, 1.0, 0.0), tiles[s])
        upper = []
        for i in range(STEP):
            acc = row_spread(own, i)
            for m in range(i):
                acc = acc - low[i, m] * upper[m]
            upper.append(acc * inv[i])
        done = upper[0]
        for i in range(1, STEP):
            done = jnp.where(sub == i, upper[i], done)
        result.append(jnp.where(lane < first + STEP, done, 0.0))
        full = None
        for t in range(s + 1, len(tiles)):
            cols = [lane_spread(tiles[t], first + k) for k in range(STEP)]
            acc = jnp.where(inside, 0.0, tiles[t])
            if t == s + 1:
                mine = []
                for k in range(STEP):
                    col = cols[k]
                    for m in range(k):
                        col = col - low[k, m] * mine[m]
                    mine.append(col * inv[k])
                    acc = acc - mine[k] * upper[k]
            else:
                if full is None:
                    full = [None] * STEP
                    for i in reversed(range(STEP)):
                        back = upper[i]
                        for m in range(i + 1, STEP):
                            back = back - low[m, i] * full[m]
                        full[i] = back * inv[i]
                for k in range(STEP):
                    acc = acc - cols[k] * full[k]
            tiles[t] = acc
        if jobs:
            jobs.pop(0)()
    for job in jobs:
        job()
    return jnp.concatenate(result, axis=0)


def factor_kernel(points_ref, gathered_ref, target_ref, factor_ref, diag_ref, work, squares):
    rows, width = factor_ref.shape
    dim = gathered_ref.shape[1] // 2
    piv = width // 2
    scale = (2.0 / (1.65 * dim)) ** 0.5

    received = jnp.concatenate(thirds(gathered_ref[...] * scale), axis=1)
    target = target_ref[...].T
    place = lax.broadcasted_iota(jnp.int32, (piv, received.shape[0]), 1).astype(jnp.float32)
    parts = []
    for b in range(2):
        chosen = jnp.where(place == target[:, b : b + 1], 1.0, 0.0).astype(jnp.bfloat16)
        found = nn_dot(chosen, received)
        found = found[:, : 2 * dim] + found[:, 2 * dim : 4 * dim] + found[:, 4 * dim :]
        parts.append(found[:, b * dim : (b + 1) * dim])
    piv_left, piv_right = exponent_operands(jnp.concatenate(parts, axis=0), True, True)

    work[:width, :] = jnp.exp(nt_dot(piv_left, piv_right))

    def kernel_rows(first):
        def job():
            work[width + first : width + first + CHUNK, :] = jnp.exp(
                nt_dot(points_ref[first : first + CHUNK, :], piv_right)
            )

        return job

    def block_job(inverse, rights, block, start):
        def job():
            at = slice(block * PANEL, (block + 1) * PANEL)
            new = nt_dot(left_form(work[at, start : start + PANEL]), inverse)
            rights.append(right_form(new))
            left = left_form(new)
            for n, right in enumerate(rights):
                to = slice(start + PANEL * (n + 1), start + PANEL * (n + 2))
                work[at, to] = work[at, to] - nt_dot(left, right)

        return job

    def rows_job(inverse, rights, first, start):
        def job():
            at = slice(width + first, width + first + CHUNK)
            new = nt_dot(left_form(work[at, start : start + PANEL]), inverse)
            here = slice(first, first + CHUNK)
            factor_ref[here, start : start + PANEL] = new.astype(jnp.bfloat16)
            squares[here, :] = new * new if start == 0 else squares[here, :] + new * new
            if rights:
                work[at, start + PANEL :] = work[at, start + PANEL :] - nt_dot(
                    left_form(new), jnp.concatenate(rights, axis=0)
                )

        return job

    jobs = [kernel_rows(first) for first in range(0, rows, CHUNK)]
    for start in range(0, width, PANEL):
        block = slice(start, start + PANEL)
        inverse = right_form(
            panel_inverse([work[start + r : start + r + STEP, block] for r in range(0, PANEL, STEP)], jobs)
        )
        rights = []
        jobs = [
            block_job(inverse, rights, n, start)
            for n in range(start // PANEL + 1, width // PANEL)
        ]
        if jobs:
            jobs.pop(0)()
        jobs += [rows_job(inverse, rights, first, start) for first in range(0, rows, CHUNK)]
    for job in jobs:
        job()
    ones = jnp.ones((STEP, 3 * PANEL), jnp.bfloat16)
    sums = nt_dot(ones, jnp.concatenate(thirds(squares[...]), axis=1))
    diag_ref[...] = 1.0 - sums[:1]


def prepare_kernel(ndev, points_ref, pivots_ref, out_ref, buffer_ref, target_ref):
    dim, rows = points_ref.shape
    blocks, piv = pivots_ref.shape
    slots = buffer_ref.shape[1]
    me = lax.axis_index("rows")
    points = points_ref[...].T
    scale = (2.0 / (1.65 * dim)) ** 0.5
    out_ref[...] = exponent_operands(points * scale, True, False)[0]
    exact = jnp.concatenate(thirds(points), axis=1)
    before = jnp.where(
        lax.broadcasted_iota(jnp.int32, (piv, piv), 0)
        < lax.broadcasted_iota(jnp.int32, (piv, piv), 1),
        1.0,
        0.0,
    ).astype(jnp.bfloat16)
    device = lax.broadcasted_iota(jnp.int32, (ndev, piv), 0)
    targets = []
    picked = []
    for b in range(blocks):
        pivots = pivots_ref[b : b + 1, :]
        low = device * rows
        owned = jnp.where((pivots >= low) & (pivots < low + rows), 1.0, 0.0)
        count = nn_dot(owned.astype(jnp.bfloat16), before)
        slot = jnp.sum(owned * count, axis=0, keepdims=True)
        owner = jnp.sum(owned * device.astype(jnp.float32), axis=0, keepdims=True)
        targets.append(owner * slots + slot)
        local = pivots - me * rows
        mine = (local >= 0) & (local < rows)
        wanted = mine & (
            lax.broadcasted_iota(jnp.int32, (slots, piv), 0).astype(jnp.float32) == slot
        )
        column = jnp.sum(
            jnp.where(wanted, (local + 1).astype(jnp.float32), 0.0), axis=1, keepdims=True
        )
        place = lax.broadcasted_iota(jnp.int32, (slots, rows), 1).astype(jnp.float32)
        chosen = jnp.where(place + 1.0 == column, 1.0, 0.0).astype(jnp.bfloat16)
        found = nn_dot(chosen, exact)
        picked.append(found[:, :dim] + found[:, dim : 2 * dim] + found[:, 2 * dim :])
    buffer_ref[...] = jnp.broadcast_to(
        jnp.concatenate(picked, axis=1)[None], buffer_ref.shape
    )
    target_ref[...] = jnp.concatenate(
        targets + [jnp.zeros((STEP - blocks, piv), jnp.float32)], axis=0
    )


VMEM = pl.BlockSpec(memory_space=pltpu.VMEM)


def prepare(points_t, pivots, ndev, slots):
    dim, rows = points_t.shape
    return pl.pallas_call(
        functools.partial(prepare_kernel, ndev),
        out_shape=[
            jax.ShapeDtypeStruct((rows, 256), jnp.bfloat16),
            jax.ShapeDtypeStruct((ndev, slots, 2 * dim), jnp.float32),
            jax.ShapeDtypeStruct((STEP, pivots.shape[1]), jnp.float32),
        ],
        in_specs=[VMEM, VMEM],
        out_specs=[VMEM, VMEM, VMEM],
        compiler_params=pltpu.CompilerParams(vmem_limit_bytes=32 * 2**20),
    )(points_t, pivots)


def factorize(points, gathered, target, width):
    rows = points.shape[0]
    return pl.pallas_call(
        factor_kernel,
        out_shape=[
            jax.ShapeDtypeStruct((rows, width), jnp.bfloat16),
            jax.ShapeDtypeStruct((1, rows), jnp.float32),
        ],
        in_specs=[VMEM, VMEM, VMEM],
        out_specs=[VMEM, VMEM],
        scratch_shapes=[
            pltpu.VMEM((width + rows, width), jnp.float32),
            pltpu.VMEM((rows, PANEL), jnp.float32),
        ],
        compiler_params=pltpu.CompilerParams(vmem_limit_bytes=48 * 2**20),
    )(points, gathered, target)


def body(points_t, pivots):
    ndev = lax.axis_size("rows")
    dim, rows_here = points_t.shape
    blocks, piv = pivots.shape
    slots = -(-(piv // ndev + 2) // STEP) * STEP
    points, buffer, target = prepare(points_t, pivots, ndev, slots)
    gathered = lax.all_to_all(buffer, "rows", 0, 0, tiled=True)
    factor, diag = factorize(
        points, gathered.reshape(ndev * slots, blocks * dim), target, blocks * piv
    )
    return (factor, diag.reshape(rows_here))


def solution(mesh):
    return jax.shard_map(
        body,
        mesh=mesh,
        in_specs=(P(None, "rows"), P()),
        out_specs=(P("rows", None), P("rows")),
        check_vma=False,
    )
```

time: 46.9 us -> 38.7 us (0.83)
  blocking collectives: 0 us -> 17.7 us
  starting transfers between devices: 9.68 us -> 0 us
  waiting for transfers between devices: 8.61 us -> 0 us
  Pallas kernels: 22.1 us -> 18.5 us
  matrix products: 2.95 us -> 0 us
  other arithmetic: 0.77 us -> 0 us
    all_to_all x0 -> x1, blocking collectives: none -> 17.7 us  [body(): gathered = lax.all_to_all(buffer, 'rows', 0, 0, tiled=True)]
    ppermute x7 -> x0, starting transfers between devices: 9.68 us -> none  [gather_relative(): pieces.append(lax.ppermute(held, 'rows', pairs))]
    ppermute x7 -> x0, waiting for transfers between devices: 8.61 us -> none  [gather_relative(): pieces.append(lax.ppermute(held, 'rows', pairs))]
    pallas_call x1, Pallas kernels: 21.7 us -> 17.8 us  [factorize(): pl.pallas_call(factor_kernel, out_shape=[jax.ShapeDtypeStruct((rows, widt...]
    dot_general x3 -> x0, matrix products: 2.95 us -> none  [the longest x2 1.67 us: body(): lax.dot_general(placer[b], gathered[:, b * dim:(b + 1) * dim], (((0,), (0...]
    reduce_sum x2 -> x0, other arithmetic: 0.52 us -> none  [the longest x1 0.27 us: body(): slot = jnp.sum(jnp.where(same, 1, 0), axis=2).astype(jnp.int32)]
    unnamed x11 -> x4, local copies, waits for them, and re-layouts: 1.6 us -> 1.62 us
  transfers between devices with their start and end apart: 7 -> 0, of which waited for: 4 -> 0; matrix products, arithmetic and copies ran while one was open for 0% -> 0% of each run, Pallas kernels for 1% -> 0%
where the time goes in v1:
time: 38.7 us; the launch traced here: 38.5 us
  Pallas kernels  18.5 us (48%)
  blocking collectives  17.7 us (46%)
  local copies, waits for them, and re-layouts  1.62 us (4%)
  between operations  0.65 us (2%)
    pallas_call x1, Pallas kernels, factorize(): pl.pallas_call(factor_kernel, out_shape=[jax.ShapeDtypeStruct((rows, widt...  17.8 us
    all_to_all x1, blocking collectives, body(): gathered = lax.all_to_all(buffer, 'rows', 0, 0, tiled=True)  17.7 us
    unnamed x4, local copies, waits for them, and re-layouts  1.62 us

profile of v1, /device:TPU:0, one launch (start us, length us, event | category | flops | bytes accessed | tf_op | source)
XLA Modules:
  0.0 38.5 jit_solution(15313449967444029376)
XLA Ops:
  0.6 0.0 copy-start
  0.6 0.9 %copy-done = f32[64,1024]{1,0:T(8,128)S(1)} copy-done((f32[64,1024]{1,0:T(8,128)S(1)}, f32[64,1024]{1,0:T(8,128)}, u32[]{:S(2)}) %copy-start) | copy-done | bytes 262168
  1.6 0.0 copy-start.1
  1.6 0.7 %copy-done.1 = s32[2,256]{1,0:T(2,128)S(1)} copy-done((s32[2,256]{1,0:T(2,128)S(1)}, s32[2,256]{1,0:T(2,128)}, u32[]{:S(2)}) %copy-start.1) | copy-done | bytes 2072
  2.3 0.7 %shard_map.41 = (bf16[1024,256]{1,0:T(8,128)(2,1)S(1)}, f32[32,16,128]{2,1,0:T(8,128)S(1)}, f32[8,256]{1,0:T(8,128)S(1)}) custom-call(f32[64,1024]{1,0:T(8,128)S(1)} %copy-done, s32[2,256]{1,0:T(2,128)S(1)} %copy-done.1), custom_call_target="tpu_custom_call" | custom-call | tf_op jit(solution)/shard_map/pallas_call | solution.py:264
  3.0 17.7 %all_to_all.5 = f32[32,16,128]{2,1,0:T(8,128)S(1)} all-to-all(f32[32,16,128]{2,1,0:T(8,128)S(1)} %get-tuple-element.8), channel_id=1, replica_groups=mesh['rows'=32] {'rows'}, dimensions={0} | all-to-all | bytes 524288 | tf_op jit(solution)/shard_map/all_to_all | solution.py:301
  20.7 17.8 %shard_map.42 = (bf16[1024,512]{1,0:T(8,128)(2,1)}, f32[1,1024]{1,0:T(1,128)}) custom-call(bf16[1024,256]{1,0:T(8,128)(2,1)S(1)} %get-tuple-element.7.points_ref, f32[512,128]{1,0:T(8,128)S(1)} %bitcast.2, f32[8,256]{1,0:T(8,128)S(1)} %get-tuple-element.9.target_ref), custom_call_target="tpu_custom_call" | custom-call | tf_op jit(solution)/shard_map/pallas_call | solution.py:279
Async XLA Ops:
  0.6 1.0 %copy-start = (f32[64,1024]{1,0:T(8,128)S(1)}, f32[64,1024]{1,0:T(8,128)}, u32[]{:S(2)}) copy-start(f32[64,1024]{1,0:T(8,128)} %points_ref.1) | copy-start | bytes 786436
  1.6 0.7 %copy-start.1 = (s32[2,256]{1,0:T(2,128)S(1)}, s32[2,256]{1,0:T(2,128)}, u32[]{:S(2)}) copy-start(s32[2,256]{1,0:T(2,128)} %pivots_ref.1) | copy-start | bytes 6148

commit v2 on v1

--- a/solution.py
+++ b/solution.py
@@ -70,16 +70,21 @@
     low = {}
     inv = {}
     for k in range(0, STEP, 2):
-        det = e[k, k] * e[k + 1, k + 1] - e[k + 1, k] * e[k + 1, k]
-        inv[k] = lax.rsqrt(e[k, k])
-        inv[k + 1] = e[k, k] * lax.rsqrt(e[k, k] * det)
-        low[k + 1, k] = e[k + 1, k] * inv[k]
-        for i in range(k + 2, STEP):
+        a, b, c = e[k, k], e[k + 1, k], e[k + 1, k + 1]
+        root = lax.rsqrt(a * c - b * b)
+        inv[k] = lax.rsqrt(a)
+        inv[k + 1] = (a * inv[k]) * root
+        low[k + 1, k] = b * inv[k]
+        over = root * root
+        rest = range(k + 2, STEP)
+        for i in rest:
             low[i, k] = e[i, k] * inv[k]
             low[i, k + 1] = (e[i, k + 1] - low[i, k] * low[k + 1, k]) * inv[k + 1]
-        for m in range(k + 2, STEP):
+        first = {i: c * e[i, k] - b * e[i, k + 1] for i in rest}
+        second = {i: a * e[i, k + 1] - b * e[i, k] for i in rest}
+        for m in rest:
             for i in range(m, STEP):
-                e[i, m] = e[i, m] - low[i, k] * low[m, k] - low[i, k + 1] * low[m, k + 1]
+                e[i, m] = e[i, m] - (first[i] * e[m, k] + second[i] * e[m, k + 1]) * over
     return low, inv
 
 
@@ -136,13 +141,14 @@
     return jnp.concatenate(result, axis=0)
 
 
-def factor_kernel(points_ref, gathered_ref, target_ref, factor_ref, diag_ref, work, squares):
+def factor_kernel(points_ref, near_ref, other_ref, target_ref, factor_ref, diag_ref, work, squares):
     rows, width = factor_ref.shape
-    dim = gathered_ref.shape[1] // 2
+    dim = near_ref.shape[1] // 2
     piv = width // 2
     scale = (2.0 / (1.65 * dim)) ** 0.5
 
-    received = jnp.concatenate(thirds(gathered_ref[...] * scale), axis=1)
+    gathered = jnp.concatenate([near_ref[...], other_ref[...]], axis=0)
+    received = jnp.concatenate(thirds(gathered * scale), axis=1)
     target = target_ref[...].T
     place = lax.broadcasted_iota(jnp.int32, (piv, received.shape[0]), 1).astype(jnp.float32)
     parts = []
@@ -153,7 +159,14 @@
         parts.append(found[:, b * dim : (b + 1) * dim])
     piv_left, piv_right = exponent_operands(jnp.concatenate(parts, axis=0), True, True)
 
-    work[:width, :] = jnp.exp(nt_dot(piv_left, piv_right))
+    def kernel_block(block):
+        def job():
+            first, last = block * PANEL, (block + 1) * PANEL
+            work[first:last, :last] = jnp.exp(nt_dot(piv_left[first:last], piv_right[:last]))
+
+        return job
+
+    kernel_block(0)()
 
     def kernel_rows(first):
         def job():
@@ -189,7 +202,8 @@
 
         return job
 
-    jobs = [kernel_rows(first) for first in range(0, rows, CHUNK)]
+    jobs = [kernel_block(block) for block in range(1, width // PANEL)]
+    jobs += [kernel_rows(first) for first in range(0, rows, CHUNK)]
     for start in range(0, width, PANEL):
         block = slice(start, start + PANEL)
         inverse = right_form(
@@ -213,12 +227,8 @@
 def prepare_kernel(ndev, points_ref, pivots_ref, out_ref, buffer_ref, target_ref):
     dim, rows = points_ref.shape
     blocks, piv = pivots_ref.shape
-    slots = buffer_ref.shape[1]
+    chips, slots = buffer_ref.shape[:2]
     me = lax.axis_index("rows")
-    points = points_ref[...].T
-    scale = (2.0 / (1.65 * dim)) ** 0.5
-    out_ref[...] = exponent_operands(points * scale, True, False)[0]
-    exact = jnp.concatenate(thirds(points), axis=1)
     before = jnp.where(
         lax.broadcasted_iota(jnp.int32, (piv, piv), 0)
         < lax.broadcasted_iota(jnp.int32, (piv, piv), 1),
@@ -226,24 +236,35 @@
         0.0,
     ).astype(jnp.bfloat16)
     device = lax.broadcasted_iota(jnp.int32, (ndev, piv), 0)
+    base = jnp.where(device % 2 == me % 2, 0, chips * slots) + device // 2 * slots
     targets = []
-    picked = []
+    columns = []
     for b in range(blocks):
         pivots = pivots_ref[b : b + 1, :]
         low = device * rows
         owned = jnp.where((pivots >= low) & (pivots < low + rows), 1.0, 0.0)
         count = nn_dot(owned.astype(jnp.bfloat16), before)
         slot = jnp.sum(owned * count, axis=0, keepdims=True)
-        owner = jnp.sum(owned * device.astype(jnp.float32), axis=0, keepdims=True)
-        targets.append(owner * slots + slot)
+        targets.append(slot + jnp.sum(owned * base.astype(jnp.float32), axis=0, keepdims=True))
         local = pivots - me * rows
         mine = (local >= 0) & (local < rows)
         wanted = mine & (
             lax.broadcasted_iota(jnp.int32, (slots, piv), 0).astype(jnp.float32) == slot
         )
-        column = jnp.sum(
-            jnp.where(wanted, (local + 1).astype(jnp.float32), 0.0), axis=1, keepdims=True
+        columns.append(
+            jnp.sum(
+                jnp.where(wanted, (local + 1).astype(jnp.float32), 0.0), axis=1, keepdims=True
+            )
         )
+    target_ref[...] = jnp.concatenate(
+        targets + [jnp.zeros((STEP - blocks, piv), jnp.float32)], axis=0
+    )
+    points = points_ref[...].T
+    scale = (2.0 / (1.65 * dim)) ** 0.5
+    out_ref[...] = exponent_operands(points * scale, True, False)[0]
+    exact = jnp.concatenate(thirds(points), axis=1)
+    picked = []
+    for column in columns:
         place = lax.broadcasted_iota(jnp.int32, (slots, rows), 1).astype(jnp.float32)
         chosen = jnp.where(place + 1.0 == column, 1.0, 0.0).astype(jnp.bfloat16)
         found = nn_dot(chosen, exact)
@@ -251,9 +272,6 @@
     buffer_ref[...] = jnp.broadcast_to(
         jnp.concatenate(picked, axis=1)[None], buffer_ref.shape
     )
-    target_ref[...] = jnp.concatenate(
-        targets + [jnp.zeros((STEP - blocks, piv), jnp.float32)], axis=0
-    )
 
 
 VMEM = pl.BlockSpec(memory_space=pltpu.VMEM)
@@ -265,16 +283,16 @@
         functools.partial(prepare_kernel, ndev),
         out_shape=[
             jax.ShapeDtypeStruct((rows, 256), jnp.bfloat16),
-            jax.ShapeDtypeStruct((ndev, slots, 2 * dim), jnp.float32),
+            jax.ShapeDtypeStruct((ndev // 2, slots, 2 * dim), jnp.float32),
             jax.ShapeDtypeStruct((STEP, pivots.shape[1]), jnp.float32),
         ],
-        in_specs=[VMEM, VMEM],
-        out_specs=[VMEM, VMEM, VMEM],
+        in_specs=[VMEM] * 2,
+        out_specs=[VMEM] * 3,
         compiler_params=pltpu.CompilerParams(vmem_limit_bytes=32 * 2**20),
     )(points_t, pivots)
 
 
-def factorize(points, gathered, target, width):
+def factorize(points, near, other, target, width):
     rows = points.shape[0]
     return pl.pallas_call(
         factor_kernel,
@@ -282,14 +300,14 @@
             jax.ShapeDtypeStruct((rows, width), jnp.bfloat16),
             jax.ShapeDtypeStruct((1, rows), jnp.float32),
         ],
-        in_specs=[VMEM, VMEM, VMEM],
-        out_specs=[VMEM, VMEM],
+        in_specs=[VMEM] * 4,
+        out_specs=[VMEM] * 2,
         scratch_shapes=[
             pltpu.VMEM((width + rows, width), jnp.float32),
             pltpu.VMEM((rows, PANEL), jnp.float32),
         ],
         compiler_params=pltpu.CompilerParams(vmem_limit_bytes=48 * 2**20),
-    )(points, gathered, target)
+    )(points, near, other, target)
 
 
 def body(points_t, pivots):
@@ -298,10 +316,11 @@
     blocks, piv = pivots.shape
     slots = -(-(piv // ndev + 2) // STEP) * STEP
     points, buffer, target = prepare(points_t, pivots, ndev, slots)
-    gathered = lax.all_to_all(buffer, "rows", 0, 0, tiled=True)
-    factor, diag = factorize(
-        points, gathered.reshape(ndev * slots, blocks * dim), target, blocks * piv
-    )
+    cores = [[d for d in range(ndev) if d % 2 == core] for core in range(2)]
+    near = lax.all_to_all(buffer, "rows", 0, 0, axis_index_groups=cores, tiled=True)
+    near = near.reshape(ndev // 2 * slots, blocks * dim)
+    other = lax.ppermute(near, "rows", [(d, d ^ 1) for d in range(ndev)])
+    factor, diag = factorize(points, near, other, target, blocks * piv)
     return (factor, diag.reshape(rows_here))
 
 

time: 38.7 us -> 38.4 us (level)
  blocking collectives: 17.7 us -> 15.9 us
  waiting for transfers between devices: 0 us -> 1.35 us
    all_to_all x1, blocking collectives: 17.7 us -> 15.9 us  [body(): lax.all_to_all(buffer, 'rows', 0, 0, axis_index_groups=cores, tiled=True)]
    ppermute x0 -> x1, waiting for transfers between devices: none -> 1.35 us  [body(): other = lax.ppermute(near, 'rows', [(d, d ^ 1) for d in range(ndev)])]
  transfers between devices with their start and end apart: 0 -> 1, of which waited for: 0 -> 1; matrix products, arithmetic and copies ran while one was open for 0% -> 0% of each run, Pallas kernels for 0% -> 0%
where the time goes in v2:
time: 38.4 us; the launch traced here: 38.2 us
  Pallas kernels  18.7 us (49%)
  blocking collectives  15.9 us (41%)
  local copies, waits for them, and re-layouts  1.62 us (4%)
  waiting for transfers between devices  1.35 us (4%)
  between operations  0.65 us (2%)
    pallas_call x1, Pallas kernels, factorize(): pl.pallas_call(factor_kernel, out_shape=[jax.ShapeDtypeStruct((rows, widt...  17.9 us
    all_to_all x1, blocking collectives, body(): lax.all_to_all(buffer, 'rows', 0, 0, axis_index_groups=cores, tiled=True)  15.9 us
    unnamed x4, local copies, waits for them, and re-layouts  1.62 us
    ppermute x1, waiting for transfers between devices, body(): other = lax.ppermute(near, 'rows', [(d, d ^ 1) for d in range(ndev)])  1.35 us
  transfers between devices with their start and end apart: 1, of which 1 were waited for; matrix products, arithmetic and copies ran while one was open for 0% of the time, Pallas kernels for 0%

profile of v2, /device:TPU:0, one launch (start us, length us, event | category | flops | bytes accessed | tf_op | source)
XLA Modules:
  0.0 38.2 jit_solution(10292656170819086302)
XLA Ops:
  0.6 0.0 copy-start
  0.6 0.9 %copy-done = f32[64,1024]{1,0:T(8,128)S(1)} copy-done((f32[64,1024]{1,0:T(8,128)S(1)}, f32[64,1024]{1,0:T(8,128)}, u32[]{:S(2)}) %copy-start) | copy-done | bytes 262168
  1.6 0.0 copy-start.1
  1.6 0.7 %copy-done.1 = s32[2,256]{1,0:T(2,128)S(1)} copy-done((s32[2,256]{1,0:T(2,128)S(1)}, s32[2,256]{1,0:T(2,128)}, u32[]{:S(2)}) %copy-start.1) | copy-done | bytes 2072
  2.3 0.8 %shard_map.41 = (bf16[1024,256]{1,0:T(8,128)(2,1)S(1)}, f32[16,16,128]{2,1,0:T(8,128)S(1)}, f32[8,256]{1,0:T(8,128)S(1)}) custom-call(f32[64,1024]{1,0:T(8,128)S(1)} %copy-done, s32[2,256]{1,0:T(2,128)S(1)} %copy-done.1), custom_call_target="tpu_custom_call" | custom-call | tf_op jit(solution)/shard_map/pallas_call | solution.py:282
  3.0 15.9 %all_to_all.5 = f32[16,16,128]{2,1,0:T(8,128)S(1)} all-to-all(f32[16,16,128]{2,1,0:T(8,128)S(1)} %get-tuple-element.8), channel_id=1, replica_groups={{0,2,4,6,8,10,12,14,16,18,20,22,24,26,28,30},{1,3,5,7,9,11,13,15,17,19,..., dimensions={0} | all-to-all | bytes 262144 | tf_op jit(solution)/shard_map/all_to_all | solution.py:320
  18.9 0.0 collective-permute-start
  18.9 1.3 %collective-permute-done.other_ref = f32[256,128]{1,0:T(8,128)S(1)} collective-permute-done((f32[256,128]{1,0:T(8,128)S(1)}, f32[256,128]{1,0:T(8,128)S(1)}, u32[]{:S(2)}, u32[]{:S(2)}) %collective-permute-start) | collective-permute-done | bytes 131104 | tf_op jit(solution)/shard_map/ppermute | solution.py:322
  20.3 17.9 %shard_map.42 = (bf16[1024,512]{1,0:T(8,128)(2,1)}, f32[1,1024]{1,0:T(1,128)}) custom-call(bf16[1024,256]{1,0:T(8,128)(2,1)S(1)} %get-tuple-element.7.points_ref, f32[256,128]{1,0:T(8,128)S(1)} %bitcast.3, f32[256,128]{1,0:T(8,128)S(1)} %collective-permute-done.other_ref, f32[8,256]{1,0:T(8,128)S(1)} %get-tuple-element.9.target_ref), custom_call_target="tpu_custom_call" | custom-call | tf_op jit(solution)/shard_map/pallas_call | solution.py:297
Async XLA Ops:
  0.6 1.0 %copy-start = (f32[64,1024]{1,0:T(8,128)S(1)}, f32[64,1024]{1,0:T(8,128)}, u32[]{:S(2)}) copy-start(f32[64,1024]{1,0:T(8,128)} %points_ref.1) | copy-start | bytes 786436
  1.6 0.7 %copy-start.1 = (s32[2,256]{1,0:T(2,128)S(1)}, s32[2,256]{1,0:T(2,128)}, u32[]{:S(2)}) copy-start(s32[2,256]{1,0:T(2,128)} %pivots_ref.1) | copy-start | bytes 6148
  18.9 1.3 %collective-permute-start = (f32[256,128]{1,0:T(8,128)S(1)}, f32[256,128]{1,0:T(8,128)S(1)}, u32[]{:S(2)}, u32[]{:S(2)}) collective-permute-start(f32[256,128]{1,0:T(8,128)S(1)} %bitcast.2), channel_id=1, source_target_pairs={{0,1},{1,0},{2,3},{3,2},{4,5},{5,4},{6,7},{7,6},{8,9},{9,8},{10,11... | collective-permute-start | bytes 393224 | tf_op jit(solution)/shard_map/ppermute | solution.py:322

commit v3 on v2

--- a/solution.py
+++ b/solution.py
@@ -62,8 +62,16 @@
     return jnp.broadcast_to(x[:, lane : lane + 1], (STEP, LANES))
 
 
-def row_spread(x, row):
-    return jnp.broadcast_to(x[row : row + 1, :], (STEP, LANES))
+class Spreader:
+    def __init__(self, ref):
+        self.ref = ref
+        self.at = 0
+
+    def rows(self, x, first=0):
+        base = self.at
+        self.at += STEP
+        self.ref[base : base + STEP, :] = x
+        return {i: self.ref[pl.ds(base + i, STEP, stride=0), :] for i in range(first, STEP)}
 
 
 def small_factor(e):
@@ -88,22 +96,27 @@
     return low, inv
 
 
-def panel_inverse(tiles, jobs):
+def panel_inverse(tiles, jobs, spread):
     lane = lax.broadcasted_iota(jnp.int32, (STEP, LANES), 1)
     sub = lax.broadcasted_iota(jnp.int32, (STEP, LANES), 0)
     tiles = list(tiles)
     jobs = list(jobs)
     result = []
+    spreader = Spreader(spread)
     for s in range(len(tiles)):
         first = STEP * s
         inside = (lane >= first) & (lane < first + STEP)
         cols = [lane_spread(tiles[s], first + k) for k in range(STEP)]
-        e = {(i, k): row_spread(cols[k], i) for k in range(STEP) for i in range(k, STEP)}
+        e = {}
+        for k in range(STEP):
+            for i, row in spreader.rows(cols[k], k).items():
+                e[i, k] = row
         low, inv = small_factor(e)
         own = jnp.where(inside, jnp.where(lane - first == sub, 1.0, 0.0), tiles[s])
         upper = []
+        own_rows = spreader.rows(own)
         for i in range(STEP):
-            acc = row_spread(own, i)
+            acc = own_rows[i]
             for m in range(i):
                 acc = acc - low[i, m] * upper[m]
             upper.append(acc * inv[i])
@@ -141,7 +154,17 @@
     return jnp.concatenate(result, axis=0)
 
 
-def factor_kernel(points_ref, near_ref, other_ref, target_ref, factor_ref, diag_ref, work, squares):
+def rounds_of(ndev):
+    rounds = [(2, 1)]
+    stride = 2
+    while stride < ndev:
+        radix = 4 if ndev // stride % 4 == 0 else 2
+        rounds.append((radix, stride))
+        stride *= radix
+    return rounds[::-1]
+
+
+def factor_kernel(points_ref, near_ref, other_ref, target_ref, factor_ref, diag_ref, work, squares, spread):
     rows, width = factor_ref.shape
     dim = near_ref.shape[1] // 2
     piv = width // 2
@@ -207,7 +230,11 @@
     for start in range(0, width, PANEL):
         block = slice(start, start + PANEL)
         inverse = right_form(
-            panel_inverse([work[start + r : start + r + STEP, block] for r in range(0, PANEL, STEP)], jobs)
+            panel_inverse(
+                [work[start + r : start + r + STEP, block] for r in range(0, PANEL, STEP)],
+                jobs,
+                spread,
+            )
         )
         rights = []
         jobs = [
@@ -227,7 +254,7 @@
 def prepare_kernel(ndev, points_ref, pivots_ref, out_ref, buffer_ref, target_ref):
     dim, rows = points_ref.shape
     blocks, piv = pivots_ref.shape
-    chips, slots = buffer_ref.shape[:2]
+    slots = buffer_ref.shape[0]
     me = lax.axis_index("rows")
     before = jnp.where(
         lax.broadcasted_iota(jnp.int32, (piv, piv), 0)
@@ -236,7 +263,11 @@
         0.0,
     ).astype(jnp.bfloat16)
     device = lax.broadcasted_iota(jnp.int32, (ndev, piv), 0)
-    base = jnp.where(device % 2 == me % 2, 0, chips * slots) + device // 2 * slots
+    base = jnp.zeros_like(device)
+    scale = slots
+    for radix, stride in rounds_of(ndev):
+        base = base + ((device // stride) ^ (me // stride)) % radix * scale
+        scale = scale * radix
     targets = []
     columns = []
     for b in range(blocks):
@@ -269,9 +300,7 @@
         chosen = jnp.where(place + 1.0 == column, 1.0, 0.0).astype(jnp.bfloat16)
         found = nn_dot(chosen, exact)
         picked.append(found[:, :dim] + found[:, dim : 2 * dim] + found[:, 2 * dim :])
-    buffer_ref[...] = jnp.broadcast_to(
-        jnp.concatenate(picked, axis=1)[None], buffer_ref.shape
-    )
+    buffer_ref[...] = jnp.concatenate(picked, axis=1)
 
 
 VMEM = pl.BlockSpec(memory_space=pltpu.VMEM)
@@ -283,7 +312,7 @@
         functools.partial(prepare_kernel, ndev),
         out_shape=[
             jax.ShapeDtypeStruct((rows, 256), jnp.bfloat16),
-            jax.ShapeDtypeStruct((ndev // 2, slots, 2 * dim), jnp.float32),
+            jax.ShapeDtypeStruct((slots, 2 * dim), jnp.float32),
             jax.ShapeDtypeStruct((STEP, pivots.shape[1]), jnp.float32),
         ],
         in_specs=[VMEM] * 2,
@@ -305,6 +334,7 @@
         scratch_shapes=[
             pltpu.VMEM((width + rows, width), jnp.float32),
             pltpu.VMEM((rows, PANEL), jnp.float32),
+            pltpu.VMEM(((STEP + 1) * PANEL, LANES), jnp.float32),
         ],
         compiler_params=pltpu.CompilerParams(vmem_limit_bytes=48 * 2**20),
     )(points, near, other, target)
@@ -316,10 +346,15 @@
     blocks, piv = pivots.shape
     slots = -(-(piv // ndev + 2) // STEP) * STEP
     points, buffer, target = prepare(points_t, pivots, ndev, slots)
-    cores = [[d for d in range(ndev) if d % 2 == core] for core in range(2)]
-    near = lax.all_to_all(buffer, "rows", 0, 0, axis_index_groups=cores, tiled=True)
-    near = near.reshape(ndev // 2 * slots, blocks * dim)
-    other = lax.ppermute(near, "rows", [(d, d ^ 1) for d in range(ndev)])
+    held = buffer
+    for radix, stride in rounds_of(ndev):
+        pieces = [held]
+        for step in range(1, radix):
+            pairs = [(d, d ^ (step * stride)) for d in range(ndev)]
+            pieces.append(lax.ppermute(held, "rows", pairs))
+        if stride > 1:
+            held = jnp.concatenate(pieces, axis=0)
+    near, other = pieces
     factor, diag = factorize(points, near, other, target, blocks * piv)
     return (factor, diag.reshape(rows_here))
 

time: 38.4 us -> 37.1 us (0.966)
  blocking collectives: 15.9 us -> 0 us
  starting transfers between devices: 0.01 us -> 9.38 us
  waiting for transfers between devices: 1.35 us -> 8.64 us
  Pallas kernels: 18.7 us -> 16.6 us
    all_to_all x1 -> x0, blocking collectives: 15.9 us -> none  [body(): lax.all_to_all(buffer, 'rows', 0, 0, axis_index_groups=cores, tiled=True)]
    ppermute x1 -> x7, starting transfers between devices: 0.01 us -> 9.38 us  [body(): pieces.append(lax.ppermute(held, 'rows', pairs))]
    ppermute x1 -> x7, waiting for transfers between devices: 1.35 us -> 8.64 us  [body(): pieces.append(lax.ppermute(held, 'rows', pairs))]
    pallas_call x1, Pallas kernels: 17.9 us -> 15.9 us  [factorize(): pl.pallas_call(factor_kernel, out_shape=[jax.ShapeDtypeStruct((rows, widt...]
    unnamed x4 -> x9, local copies, waits for them, and re-layouts: 1.62 us -> 1.64 us
  transfers between devices with their start and end apart: 1 -> 7, of which waited for: 1 -> 5; matrix products, arithmetic and copies ran while one was open for 0% -> 0% of each run, Pallas kernels for 0% -> 0%
where the time goes in v3:
time: 37.1 us; the launch traced here: 36.9 us
  Pallas kernels  16.6 us (45%)
  starting transfers between devices  9.38 us (25%)
  waiting for transfers between devices  8.64 us (23%)
  local copies, waits for them, and re-layouts  1.64 us (4%)
  between operations  0.67 us (2%)
    pallas_call x1, Pallas kernels, factorize(): pl.pallas_call(factor_kernel, out_shape=[jax.ShapeDtypeStruct((rows, widt...  15.9 us
    ppermute x7, starting transfers between devices, body(): pieces.append(lax.ppermute(held, 'rows', pairs))  9.38 us
    ppermute x7, waiting for transfers between devices, body(): pieces.append(lax.ppermute(held, 'rows', pairs))  8.64 us
    unnamed x9, local copies, waits for them, and re-layouts  1.64 us
  transfers between devices with their start and end apart: 7, of which 5 were waited for; matrix products, arithmetic and copies ran while one was open for 0% of the time, Pallas kernels for 0%

profile of v3, /device:TPU:0, one launch (start us, length us, event | category | flops | bytes accessed | tf_op | source)
XLA Modules:
  0.0 36.9 jit_solution(14235620905697973741)
XLA Ops:
  0.6 0.0 copy-start
  0.6 0.9 %copy-done = f32[64,1024]{1,0:T(8,128)S(1)} copy-done((f32[64,1024]{1,0:T(8,128)S(1)}, f32[64,1024]{1,0:T(8,128)}, u32[]{:S(2)}) %copy-start) | copy-done | bytes 262168
  1.6 0.0 copy-start.1
  1.6 0.7 %copy-done.1 = s32[2,256]{1,0:T(2,128)S(1)} copy-done((s32[2,256]{1,0:T(2,128)S(1)}, s32[2,256]{1,0:T(2,128)}, u32[]{:S(2)}) %copy-start.1) | copy-done | bytes 2072
  2.3 0.7 %shard_map.41 = (bf16[1024,256]{1,0:T(8,128)(2,1)S(1)}, f32[16,128]{1,0:T(8,128)S(1)}, f32[8,256]{1,0:T(8,128)S(1)}) custom-call(f32[64,1024]{1,0:T(8,128)S(1)} %copy-done, s32[2,256]{1,0:T(2,128)S(1)} %copy-done.1), custom_call_target="tpu_custom_call" | custom-call | tf_op jit(solution)/shard_map/pallas_call | solution.py:311
  3.0 5.1 %collective-permute-start.2 = (f32[16,128]{1,0:T(8,128)S(1)}, f32[16,128]{1,0:T(8,128)S(1)}, u32[]{:S(2)}, u32[]{:S(2)}) collective-permute-start(f32[16,128]{1,0:T(8,128)S(1)} %get-tuple-element.8), channel_id=1, source_target_pairs={{0,24},{1,25},{2,26},{3,27},{4,28},{5,29},{6,30},{7,31},{8,16},{9,... | collective-permute-start | bytes 24584 | tf_op jit(solution)/shard_map/ppermute | solution.py:354
  8.1 0.0 collective-permute-start.1
  8.1 0.6 %collective-permute-start = (f32[16,128]{1,0:T(8,128)S(1)}, f32[16,128]{1,0:T(8,128)S(1)}, u32[]{:S(2)}, u32[]{:S(2)}) collective-permute-start(f32[16,128]{1,0:T(8,128)S(1)} %get-tuple-element.8), channel_id=1, source_target_pairs={{0,8},{1,9},{2,10},{3,11},{4,12},{5,13},{6,14},{7,15},{8,0},{9,1},... | collective-permute-start | bytes 24584 | tf_op jit(solution)/shard_map/ppermute | solution.py:354
  8.8 3.0 %collective-permute-done = f32[16,128]{1,0:T(8,128)S(1)} collective-permute-done((f32[16,128]{1,0:T(8,128)S(1)}, f32[16,128]{1,0:T(8,128)S(1)}, u32[]{:S(2)}, u32[]{:S(2)}) %collective-permute-start) | collective-permute-done | bytes 8224 | tf_op jit(solution)/shard_map/ppermute | solution.py:354
  11.8 0.9 %collective-permute-done.1 = f32[16,128]{1,0:T(8,128)S(1)} collective-permute-done((f32[16,128]{1,0:T(8,128)S(1)}, f32[16,128]{1,0:T(8,128)S(1)}, u32[]{:S(2)}, u32[]{:S(2)}) %collective-permute-start.1) | collective-permute-done | bytes 8224 | tf_op jit(solution)/shard_map/ppermute | solution.py:354
  12.7 0.0 collective-permute-done.2
  12.7 1.6 %collective-permute-start.3 = (f32[64,128]{1,0:T(8,128)S(1)}, f32[64,128]{1,0:T(8,128)S(1)}, u32[]{:S(2)}, u32[]{:S(2)}) collective-permute-start(f32[64,128]{1,0:T(8,128)S(1)} %get-tuple-element.12), channel_id=1, source_target_pairs={{0,2},{1,3},{2,0},{3,1},{4,6},{5,7},{6,4},{7,5},{8,10},{9,11},{10,... | collective-permute-start | bytes 98312 | tf_op jit(solution)/shard_map/ppermute | solution.py:354
  14.2 1.5 %collective-permute-start.5 = (f32[64,128]{1,0:T(8,128)S(1)}, f32[64,128]{1,0:T(8,128)S(1)}, u32[]{:S(2)}, u32[]{:S(2)}) collective-permute-start(f32[64,128]{1,0:T(8,128)S(1)} %get-tuple-element.12), channel_id=1, source_target_pairs={{0,6},{1,7},{2,4},{3,5},{4,2},{5,3},{6,0},{7,1},{8,14},{9,15},{10,... | collective-permute-start | bytes 98312 | tf_op jit(solution)/shard_map/ppermute | solution.py:354
  15.7 0.5 %collective-permute-start.4 = (f32[64,128]{1,0:T(8,128)S(1)}, f32[64,128]{1,0:T(8,128)S(1)}, u32[]{:S(2)}, u32[]{:S(2)}) collective-permute-start(f32[64,128]{1,0:T(8,128)S(1)} %get-tuple-element.12), channel_id=1, source_target_pairs={{0,4},{1,5},{2,6},{3,7},{4,0},{5,1},{6,2},{7,3},{8,12},{9,13},{10,... | collective-permute-start | bytes 98312 | tf_op jit(solution)/shard_map/ppermute | solution.py:354
  16.2 0.4 %collective-permute-done.3 = f32[64,128]{1,0:T(8,128)S(1)} collective-permute-done((f32[64,128]{1,0:T(8,128)S(1)}, f32[64,128]{1,0:T(8,128)S(1)}, u32[]{:S(2)}, u32[]{:S(2)}) %collective-permute-start.3) | collective-permute-done | bytes 32800 | tf_op jit(solution)/shard_map/ppermute | solution.py:354
  16.7 3.0 %collective-permute-done.4 = f32[64,128]{1,0:T(8,128)S(1)} collective-permute-done((f32[64,128]{1,0:T(8,128)S(1)}, f32[64,128]{1,0:T(8,128)S(1)}, u32[]{:S(2)}, u32[]{:S(2)}) %collective-permute-start.4) | collective-permute-done | bytes 32800 | tf_op jit(solution)/shard_map/ppermute | solution.py:354
  19.6 0.0 collective-permute-done.5
  19.7 0.1 collective-permute-start.6
  19.7 1.3 %collective-permute-done.6.other_ref = f32[256,128]{1,0:T(8,128)S(1)} collective-permute-done((f32[256,128]{1,0:T(8,128)S(1)}, f32[256,128]{1,0:T(8,128)S(1)}, u32[]{:S(2)}, u32[]{:S(2)}) %collective-permute-start.6) | collective-permute-done | bytes 131104 | tf_op jit(solution)/shard_map/ppermute | solution.py:354
  21.1 15.9 %shard_map.42 = (bf16[1024,512]{1,0:T(8,128)(2,1)}, f32[1,1024]{1,0:T(1,128)}) custom-call(bf16[1024,256]{1,0:T(8,128)(2,1)S(1)} %get-tuple-element.7.points_ref, f32[256,128]{1,0:T(8,128)S(1)} %constant_dynamic-update-slice_fusion.4.near_ref, f32[256,128]{1,0:T(8,128)S(1)} %collective-permute-done.6.other_ref, f32[8,256]{1,0:T(8,128)S(1)} %get-tuple-element.9.target_ref), custom_call_target="tpu_custom_call" | custom-call | tf_op jit(solution)/shard_map/pallas_call | solution.py:326
  (7 shorter events, 0.0 us)
Async XLA Ops:
  0.6 1.0 %copy-start = (f32[64,1024]{1,0:T(8,128)S(1)}, f32[64,1024]{1,0:T(8,128)}, u32[]{:S(2)}) copy-start(f32[64,1024]{1,0:T(8,128)} %points_ref.1) | copy-start | bytes 786436
  1.6 0.7 %copy-start.1 = (s32[2,256]{1,0:T(2,128)S(1)}, s32[2,256]{1,0:T(2,128)}, u32[]{:S(2)}) copy-start(s32[2,256]{1,0:T(2,128)} %pivots_ref.1) | copy-start | bytes 6148
  3.0 9.7 %collective-permute-start.2 = (f32[16,128]{1,0:T(8,128)S(1)}, f32[16,128]{1,0:T(8,128)S(1)}, u32[]{:S(2)}, u32[]{:S(2)}) collective-permute-start(f32[16,128]{1,0:T(8,128)S(1)} %get-tuple-element.8), channel_id=1, source_target_pairs={{0,24},{1,25},{2,26},{3,27},{4,28},{5,29},{6,30},{7,31},{8,16},{9,... | collective-permute-start | bytes 24584 | tf_op jit(solution)/shard_map/ppermute | solution.py:354
  8.1 4.5 %collective-permute-start.1 = (f32[16,128]{1,0:T(8,128)S(1)}, f32[16,128]{1,0:T(8,128)S(1)}, u32[]{:S(2)}, u32[]{:S(2)}) collective-permute-start(f32[16,128]{1,0:T(8,128)S(1)} %get-tuple-element.8), channel_id=1, source_target_pairs={{0,16},{1,17},{2,18},{3,19},{4,20},{5,21},{6,22},{7,23},{8,24},{9,... | collective-permute-start | bytes 24584 | tf_op jit(solution)/shard_map/ppermute | solution.py:354
  8.1 3.7 %collective-permute-start = (f32[16,128]{1,0:T(8,128)S(1)}, f32[16,128]{1,0:T(8,128)S(1)}, u32[]{:S(2)}, u32[]{:S(2)}) collective-permute-start(f32[16,128]{1,0:T(8,128)S(1)} %get-tuple-element.8), channel_id=1, source_target_pairs={{0,8},{1,9},{2,10},{3,11},{4,12},{5,13},{6,14},{7,15},{8,0},{9,1},... | collective-permute-start | bytes 24584 | tf_op jit(solution)/shard_map/ppermute | solution.py:354
  12.7 4.0 %collective-permute-start.3 = (f32[64,128]{1,0:T(8,128)S(1)}, f32[64,128]{1,0:T(8,128)S(1)}, u32[]{:S(2)}, u32[]{:S(2)}) collective-permute-start(f32[64,128]{1,0:T(8,128)S(1)} %get-tuple-element.12), channel_id=1, source_target_pairs={{0,2},{1,3},{2,0},{3,1},{4,6},{5,7},{6,4},{7,5},{8,10},{9,11},{10,... | collective-permute-start | bytes 98312 | tf_op jit(solution)/shard_map/ppermute | solution.py:354
  14.2 5.4 %collective-permute-start.5 = (f32[64,128]{1,0:T(8,128)S(1)}, f32[64,128]{1,0:T(8,128)S(1)}, u32[]{:S(2)}, u32[]{:S(2)}) collective-permute-start(f32[64,128]{1,0:T(8,128)S(1)} %get-tuple-element.12), channel_id=1, source_target_pairs={{0,6},{1,7},{2,4},{3,5},{4,2},{5,3},{6,0},{7,1},{8,14},{9,15},{10,... | collective-permute-start | bytes 98312 | tf_op jit(solution)/shard_map/ppermute | solution.py:354
  15.7 3.9 %collective-permute-start.4 = (f32[64,128]{1,0:T(8,128)S(1)}, f32[64,128]{1,0:T(8,128)S(1)}, u32[]{:S(2)}, u32[]{:S(2)}) collective-permute-start(f32[64,128]{1,0:T(8,128)S(1)} %get-tuple-element.12), channel_id=1, source_target_pairs={{0,4},{1,5},{2,6},{3,7},{4,0},{5,1},{6,2},{7,3},{8,12},{9,13},{10,... | collective-permute-start | bytes 98312 | tf_op jit(solution)/shard_map/ppermute | solution.py:354
  19.7 1.4 %collective-permute-start.6 = (f32[256,128]{1,0:T(8,128)S(1)}, f32[256,128]{1,0:T(8,128)S(1)}, u32[]{:S(2)}, u32[]{:S(2)}) collective-permute-start(f32[256,128]{1,0:T(8,128)S(1)} %constant_dynamic-update-slice_fusion.4.near_ref), channel_id=1, source_target_pairs={{0,1},{1,0},{2,3},{3,2},{4,5},{5,4},{6,7},{7,6},{8,9},{9,8},{10,11... | collective-permute-start | bytes 393224 | tf_op jit(solution)/shard_map/ppermute | solution.py:354

commit v4 on v3

--- a/solution.py
+++ b/solution.py
@@ -154,16 +154,6 @@
     return jnp.concatenate(result, axis=0)
 
 
-def rounds_of(ndev):
-    rounds = [(2, 1)]
-    stride = 2
-    while stride < ndev:
-        radix = 4 if ndev // stride % 4 == 0 else 2
-        rounds.append((radix, stride))
-        stride *= radix
-    return rounds[::-1]
-
-
 def factor_kernel(points_ref, near_ref, other_ref, target_ref, factor_ref, diag_ref, work, squares, spread):
     rows, width = factor_ref.shape
     dim = near_ref.shape[1] // 2
@@ -173,28 +163,36 @@
     gathered = jnp.concatenate([near_ref[...], other_ref[...]], axis=0)
     received = jnp.concatenate(thirds(gathered * scale), axis=1)
     target = target_ref[...].T
-    place = lax.broadcasted_iota(jnp.int32, (piv, received.shape[0]), 1).astype(jnp.float32)
-    parts = []
-    for b in range(2):
-        chosen = jnp.where(place == target[:, b : b + 1], 1.0, 0.0).astype(jnp.bfloat16)
-        found = nn_dot(chosen, received)
-        found = found[:, : 2 * dim] + found[:, 2 * dim : 4 * dim] + found[:, 4 * dim :]
-        parts.append(found[:, b * dim : (b + 1) * dim])
-    piv_left, piv_right = exponent_operands(jnp.concatenate(parts, axis=0), True, True)
+    place = lax.broadcasted_iota(jnp.int32, (PANEL, received.shape[0]), 1).astype(jnp.float32)
+    piv_left = []
+    piv_right = []
 
     def kernel_block(block):
         def job():
-            first, last = block * PANEL, (block + 1) * PANEL
-            work[first:last, :last] = jnp.exp(nt_dot(piv_left[first:last], piv_right[:last]))
+            first = block * PANEL
+            half, at = divmod(first, piv)
+            chosen = jnp.where(place == target[at : at + PANEL, half : half + 1], 1.0, 0.0)
+            found = nn_dot(chosen.astype(jnp.bfloat16), received)
+            found = found[:, : 2 * dim] + found[:, 2 * dim : 4 * dim] + found[:, 4 * dim :]
+            left, right = exponent_operands(found[:, half * dim : (half + 1) * dim], True, True)
+            piv_left.append(left)
+            piv_right.append(right)
+            for n in range(block + 1):
+                work[first : first + PANEL, n * PANEL : (n + 1) * PANEL] = jnp.exp(
+                    nt_dot(left, piv_right[n])
+                )
 
         return job
 
     kernel_block(0)()
 
-    def kernel_rows(first):
+    def kernel_rows(first, pair):
         def job():
-            work[width + first : width + first + CHUNK, :] = jnp.exp(
-                nt_dot(points_ref[first : first + CHUNK, :], piv_right)
+            right = jnp.concatenate(piv_right[2 * pair : 2 * pair + 2], axis=0)
+            cols = slice(2 * pair * PANEL, 2 * (pair + 1) * PANEL)
+            here = slice(first, first + 2 * CHUNK)
+            work[width + first : width + first + 2 * CHUNK, cols] = jnp.exp(
+                nt_dot(points_ref[here, :], right)
             )
 
         return job
@@ -226,7 +224,11 @@
         return job
 
     jobs = [kernel_block(block) for block in range(1, width // PANEL)]
-    jobs += [kernel_rows(first) for first in range(0, rows, CHUNK)]
+    jobs += [
+        kernel_rows(first, pair)
+        for pair in range(width // PANEL // 2)
+        for first in range(0, rows, 2 * CHUNK)
+    ]
     for start in range(0, width, PANEL):
         block = slice(start, start + PANEL)
         inverse = right_form(
@@ -246,15 +248,18 @@
         jobs += [rows_job(inverse, rights, first, start) for first in range(0, rows, CHUNK)]
     for job in jobs:
         job()
-    ones = jnp.ones((STEP, 3 * PANEL), jnp.bfloat16)
-    sums = nt_dot(ones, jnp.concatenate(thirds(squares[...]), axis=1))
-    diag_ref[...] = 1.0 - sums[:1]
-
-
-def prepare_kernel(ndev, points_ref, pivots_ref, out_ref, buffer_ref, target_ref):
-    dim, rows = points_ref.shape
+    ones = jnp.ones((3 * PANEL, LANES), jnp.bfloat16)
+    keep = lax.broadcasted_iota(jnp.int32, (LANES, LANES), 0) == lax.broadcasted_iota(
+        jnp.int32, (LANES, LANES), 1
+    )
+    for first in range(0, rows, LANES):
+        here = slice(first, first + LANES)
+        sums = nn_dot(jnp.concatenate(thirds(squares[here, :]), axis=1), ones)
+        diag_ref[:, here] = 1.0 - jnp.sum(jnp.where(keep, sums, 0.0), axis=0, keepdims=True)
+
+
+def slots_kernel(ndev, rows, slots, pivots_ref, target_ref, column_ref):
     blocks, piv = pivots_ref.shape
-    slots = buffer_ref.shape[0]
     me = lax.axis_index("rows")
     before = jnp.where(
         lax.broadcasted_iota(jnp.int32, (piv, piv), 0)
@@ -263,11 +268,7 @@
         0.0,
     ).astype(jnp.bfloat16)
     device = lax.broadcasted_iota(jnp.int32, (ndev, piv), 0)
-    base = jnp.zeros_like(device)
-    scale = slots
-    for radix, stride in rounds_of(ndev):
-        base = base + ((device // stride) ^ (me // stride)) % radix * scale
-        scale = scale * radix
+    base = jnp.where(device % 2 == me % 2, 0, ndev // 2 * slots) + device // 2 * slots
     targets = []
     columns = []
     for b in range(blocks):
@@ -290,17 +291,22 @@
     target_ref[...] = jnp.concatenate(
         targets + [jnp.zeros((STEP - blocks, piv), jnp.float32)], axis=0
     )
+    for b in range(blocks):
+        column_ref[b * slots : (b + 1) * slots, :] = jnp.broadcast_to(columns[b], (slots, LANES))
+
+
+def prepare_kernel(points_ref, column_ref, out_ref, buffer_ref):
+    dim, rows = points_ref.shape
+    slots = buffer_ref.shape[1]
     points = points_ref[...].T
     scale = (2.0 / (1.65 * dim)) ** 0.5
     out_ref[...] = exponent_operands(points * scale, True, False)[0]
-    exact = jnp.concatenate(thirds(points), axis=1)
-    picked = []
-    for column in columns:
-        place = lax.broadcasted_iota(jnp.int32, (slots, rows), 1).astype(jnp.float32)
-        chosen = jnp.where(place + 1.0 == column, 1.0, 0.0).astype(jnp.bfloat16)
-        found = nn_dot(chosen, exact)
-        picked.append(found[:, :dim] + found[:, dim : 2 * dim] + found[:, 2 * dim :])
-    buffer_ref[...] = jnp.concatenate(picked, axis=1)
+    place = lax.broadcasted_iota(jnp.int32, (column_ref.shape[0], rows), 1).astype(jnp.float32)
+    chosen = jnp.where(place + 1.0 == column_ref[:, :1], 1.0, 0.0).astype(jnp.bfloat16)
+    found = nn_dot(chosen, jnp.concatenate(thirds(points), axis=1))
+    found = found[:, :dim] + found[:, dim : 2 * dim] + found[:, 2 * dim :]
+    picked = jnp.concatenate([found[:slots], found[slots:]], axis=1)
+    buffer_ref[...] = jnp.broadcast_to(picked[None], buffer_ref.shape)
 
 
 VMEM = pl.BlockSpec(memory_space=pltpu.VMEM)
@@ -308,17 +314,31 @@
 
 def prepare(points_t, pivots, ndev, slots):
     dim, rows = points_t.shape
-    return pl.pallas_call(
-        functools.partial(prepare_kernel, ndev),
+    blocks, piv = pivots.shape
+    target, column = pl.pallas_call(
+        functools.partial(slots_kernel, ndev, rows, slots),
+        out_shape=[
+            jax.ShapeDtypeStruct((STEP, piv), jnp.float32),
+            jax.ShapeDtypeStruct((blocks * slots, LANES), jnp.float32),
+        ],
+        in_specs=[VMEM],
+        out_specs=[VMEM] * 2,
+        compiler_params=pltpu.CompilerParams(vmem_limit_bytes=32 * 2**20),
+        cost_estimate=pl.CostEstimate(
+            flops=4 * blocks * piv * piv * ndev, bytes_accessed=3 * 2**20, transcendentals=0
+        ),
+    )(pivots)
+    points, buffer = pl.pallas_call(
+        prepare_kernel,
         out_shape=[
             jax.ShapeDtypeStruct((rows, 256), jnp.bfloat16),
-            jax.ShapeDtypeStruct((slots, 2 * dim), jnp.float32),
-            jax.ShapeDtypeStruct((STEP, pivots.shape[1]), jnp.float32),
+            jax.ShapeDtypeStruct((ndev // 2, slots, blocks * dim), jnp.float32),
         ],
         in_specs=[VMEM] * 2,
-        out_specs=[VMEM] * 3,
+        out_specs=[VMEM] * 2,
         compiler_params=pltpu.CompilerParams(vmem_limit_bytes=32 * 2**20),
-    )(points_t, pivots)
+    )(points_t, column)
+    return points, buffer, target
 
 
 def factorize(points, near, other, target, width):
@@ -346,15 +366,10 @@
     blocks, piv = pivots.shape
     slots = -(-(piv // ndev + 2) // STEP) * STEP
     points, buffer, target = prepare(points_t, pivots, ndev, slots)
-    held = buffer
-    for radix, stride in rounds_of(ndev):
-        pieces = [held]
-        for step in range(1, radix):
-            pairs = [(d, d ^ (step * stride)) for d in range(ndev)]
-            pieces.append(lax.ppermute(held, "rows", pairs))
-        if stride > 1:
-            held = jnp.concatenate(pieces, axis=0)
-    near, other = pieces
+    cores = [[d for d in range(ndev) if d % 2 == core] for core in range(2)]
+    near = lax.all_to_all(buffer, "rows", 0, 0, axis_index_groups=cores, tiled=True)
+    near = near.reshape(ndev // 2 * slots, blocks * dim)
+    other = lax.ppermute(near, "rows", [(d, d ^ 1) for d in range(ndev)])
     factor, diag = factorize(points, near, other, target, blocks * piv)
     return (factor, diag.reshape(rows_here))
 

time: 37.1 us -> 36.7 us (0.989)
  blocking collectives: 0 us -> 15.9 us
  starting transfers between devices: 9.38 us -> 0.01 us
  waiting for transfers between devices: 8.64 us -> 1.35 us
  Pallas kernels: 16.6 us -> 17 us
    all_to_all x0 -> x1, blocking collectives: none -> 15.9 us  [body(): lax.all_to_all(buffer, 'rows', 0, 0, axis_index_groups=cores, tiled=True)]
    ppermute x7 -> x1, starting transfers between devices: 9.38 us -> 0.01 us  [body(): other = lax.ppermute(near, 'rows', [(d, d ^ 1) for d in range(ndev)])]
    ppermute x7 -> x1, waiting for transfers between devices: 8.64 us -> 1.35 us  [body(): other = lax.ppermute(near, 'rows', [(d, d ^ 1) for d in range(ndev)])]
    pallas_call x1 -> x2, Pallas kernels: 0.73 us -> 0.93 us  [the longest x1 0.69 us: prepare(): pl.pallas_call(prepare_kernel, out_shape=[jax.ShapeDtypeStruct((rows, 256...]
    unnamed x9 -> x4, local copies, waits for them, and re-layouts: 1.64 us -> 1.63 us
  transfers between devices with their start and end apart: 7 -> 1, of which waited for: 5 -> 1; matrix products, arithmetic and copies ran while one was open for 0% -> 0% of each run, Pallas kernels for 0% -> 0%
where the time goes in v4:
time: 36.7 us; the launch traced here: 36.5 us
  Pallas kernels  17 us (46%)
  blocking collectives  15.9 us (43%)
  local copies, waits for them, and re-layouts  1.63 us (4%)
  waiting for transfers between devices  1.35 us (4%)
  between operations  0.65 us (2%)
    pallas_call x1, Pallas kernels, factorize(): pl.pallas_call(factor_kernel, out_shape=[jax.ShapeDtypeStruct((rows, widt...  16.1 us
    all_to_all x1, blocking collectives, body(): lax.all_to_all(buffer, 'rows', 0, 0, axis_index_groups=cores, tiled=True)  15.9 us
    unnamed x4, local copies, waits for them, and re-layouts  1.63 us
    ppermute x1, waiting for transfers between devices, body(): other = lax.ppermute(near, 'rows', [(d, d ^ 1) for d in range(ndev)])  1.35 us
  transfers between devices with their start and end apart: 1, of which 1 were waited for; matrix products, arithmetic and copies ran while one was open for 0% of the time, Pallas kernels for 0%

profile of v4, /device:TPU:0, one launch (start us, length us, event | category | flops | bytes accessed | tf_op | source)
XLA Modules:
  0.0 36.5 jit_solution(17723524865752076880)
XLA Ops:
  0.6 0.0 copy-start.1
  0.6 0.7 %copy-done.1 = s32[2,256]{1,0:T(2,128)S(1)} copy-done((s32[2,256]{1,0:T(2,128)S(1)}, s32[2,256]{1,0:T(2,128)}, u32[]{:S(2)}) %copy-start.1) | copy-done | bytes 2072
  1.3 0.2 shard_map.41
  1.6 0.0 copy-start
  1.6 1.0 %copy-done = f32[64,1024]{1,0:T(8,128)S(1)} copy-done((f32[64,1024]{1,0:T(8,128)S(1)}, f32[64,1024]{1,0:T(8,128)}, u32[]{:S(2)}) %copy-start) | copy-done | bytes 262168
  2.5 0.7 %shard_map.42 = (bf16[1024,256]{1,0:T(8,128)(2,1)S(1)}, f32[16,16,128]{2,1,0:T(8,128)S(1)}) custom-call(f32[64,1024]{1,0:T(8,128)S(1)} %copy-done, f32[32,128]{1,0:T(8,128)S(1)} %get-tuple-element.8.column_ref), custom_call_target="tpu_custom_call" | custom-call | tf_op jit(solution)/shard_map/pallas_call | solution.py:331
  3.2 15.9 %all_to_all.5 = f32[16,16,128]{2,1,0:T(8,128)S(1)} all-to-all(f32[16,16,128]{2,1,0:T(8,128)S(1)} %get-tuple-element.10), channel_id=1, replica_groups={{0,2,4,6,8,10,12,14,16,18,20,22,24,26,28,30},{1,3,5,7,9,11,13,15,17,19,..., dimensions={0} | all-to-all | bytes 262144 | tf_op jit(solution)/shard_map/all_to_all | solution.py:370
  19.1 0.0 collective-permute-start
  19.1 1.3 %collective-permute-done.other_ref = f32[256,128]{1,0:T(8,128)S(1)} collective-permute-done((f32[256,128]{1,0:T(8,128)S(1)}, f32[256,128]{1,0:T(8,128)S(1)}, u32[]{:S(2)}, u32[]{:S(2)}) %collective-permute-start) | collective-permute-done | bytes 131104 | tf_op jit(solution)/shard_map/ppermute | solution.py:372
  20.5 16.1 %shard_map.43 = (bf16[1024,512]{1,0:T(8,128)(2,1)}, f32[1,1024]{1,0:T(1,128)}) custom-call(bf16[1024,256]{1,0:T(8,128)(2,1)S(1)} %get-tuple-element.9.points_ref, f32[256,128]{1,0:T(8,128)S(1)} %bitcast.3, f32[256,128]{1,0:T(8,128)S(1)} %collective-permute-done.other_ref, f32[8,256]{1,0:T(8,128)S(1)} %get-tuple-element.11.target_ref), custom_call_target="tpu_custom_call" | custom-call | tf_op jit(solution)/shard_map/pallas_call | solution.py:346
Async XLA Ops:
  0.6 0.7 %copy-start.1 = (s32[2,256]{1,0:T(2,128)S(1)}, s32[2,256]{1,0:T(2,128)}, u32[]{:S(2)}) copy-start(s32[2,256]{1,0:T(2,128)} %pivots_ref.1) | copy-start | bytes 6148
  1.6 1.0 %copy-start = (f32[64,1024]{1,0:T(8,128)S(1)}, f32[64,1024]{1,0:T(8,128)}, u32[]{:S(2)}) copy-start(f32[64,1024]{1,0:T(8,128)} %points_ref.1) | copy-start | bytes 786436
  19.1 1.3 %collective-permute-start = (f32[256,128]{1,0:T(8,128)S(1)}, f32[256,128]{1,0:T(8,128)S(1)}, u32[]{:S(2)}, u32[]{:S(2)}) collective-permute-start(f32[256,128]{1,0:T(8,128)S(1)} %bitcast.2), channel_id=1, source_target_pairs={{0,1},{1,0},{2,3},{3,2},{4,5},{5,4},{6,7},{7,6},{8,9},{9,8},{10,11... | collective-permute-start | bytes 393224 | tf_op jit(solution)/shard_map/ppermute | solution.py:372

commit v5 on v4

--- a/solution.py
+++ b/solution.py
@@ -83,16 +83,12 @@
         inv[k] = lax.rsqrt(a)
         inv[k + 1] = (a * inv[k]) * root
         low[k + 1, k] = b * inv[k]
-        over = root * root
-        rest = range(k + 2, STEP)
-        for i in rest:
+        for i in range(k + 2, STEP):
             low[i, k] = e[i, k] * inv[k]
             low[i, k + 1] = (e[i, k + 1] - low[i, k] * low[k + 1, k]) * inv[k + 1]
-        first = {i: c * e[i, k] - b * e[i, k + 1] for i in rest}
-        second = {i: a * e[i, k + 1] - b * e[i, k] for i in rest}
-        for m in rest:
+        for m in range(k + 2, STEP):
             for i in range(m, STEP):
-                e[i, m] = e[i, m] - (first[i] * e[m, k] + second[i] * e[m, k + 1]) * over
+                e[i, m] = (e[i, m] - low[i, k] * low[m, k]) - low[i, k + 1] * low[m, k + 1]
     return low, inv
 
 
@@ -295,15 +291,17 @@
         column_ref[b * slots : (b + 1) * slots, :] = jnp.broadcast_to(columns[b], (slots, LANES))
 
 
-def prepare_kernel(points_ref, column_ref, out_ref, buffer_ref):
+def points_kernel(points_ref, out_ref):
+    scale = (2.0 / (1.65 * points_ref.shape[0])) ** 0.5
+    out_ref[...] = exponent_operands(points_ref[...].T * scale, True, False)[0]
+
+
+def pick_kernel(points_ref, column_ref, buffer_ref):
     dim, rows = points_ref.shape
     slots = buffer_ref.shape[1]
-    points = points_ref[...].T
-    scale = (2.0 / (1.65 * dim)) ** 0.5
-    out_ref[...] = exponent_operands(points * scale, True, False)[0]
     place = lax.broadcasted_iota(jnp.int32, (column_ref.shape[0], rows), 1).astype(jnp.float32)
     chosen = jnp.where(place + 1.0 == column_ref[:, :1], 1.0, 0.0).astype(jnp.bfloat16)
-    found = nn_dot(chosen, jnp.concatenate(thirds(points), axis=1))
+    found = nt_dot(chosen, jnp.concatenate(thirds(points_ref[...]), axis=0))
     found = found[:, :dim] + found[:, dim : 2 * dim] + found[:, 2 * dim :]
     picked = jnp.concatenate([found[:slots], found[slots:]], axis=1)
     buffer_ref[...] = jnp.broadcast_to(picked[None], buffer_ref.shape)
@@ -324,20 +322,24 @@
         in_specs=[VMEM],
         out_specs=[VMEM] * 2,
         compiler_params=pltpu.CompilerParams(vmem_limit_bytes=32 * 2**20),
-        cost_estimate=pl.CostEstimate(
-            flops=4 * blocks * piv * piv * ndev, bytes_accessed=3 * 2**20, transcendentals=0
-        ),
     )(pivots)
-    points, buffer = pl.pallas_call(
-        prepare_kernel,
-        out_shape=[
-            jax.ShapeDtypeStruct((rows, 256), jnp.bfloat16),
-            jax.ShapeDtypeStruct((ndev // 2, slots, blocks * dim), jnp.float32),
-        ],
+    buffer = pl.pallas_call(
+        pick_kernel,
+        out_shape=jax.ShapeDtypeStruct((ndev // 2, slots, blocks * dim), jnp.float32),
         in_specs=[VMEM] * 2,
-        out_specs=[VMEM] * 2,
+        out_specs=VMEM,
         compiler_params=pltpu.CompilerParams(vmem_limit_bytes=32 * 2**20),
     )(points_t, column)
+    points = pl.pallas_call(
+        points_kernel,
+        out_shape=jax.ShapeDtypeStruct((rows, 256), jnp.bfloat16),
+        in_specs=[VMEM],
+        out_specs=VMEM,
+        compiler_params=pltpu.CompilerParams(vmem_limit_bytes=32 * 2**20),
+        cost_estimate=pl.CostEstimate(
+            flops=20 * rows * dim, bytes_accessed=3 * rows * 256, transcendentals=0
+        ),
+    )(points_t)
     return points, buffer, target
 
 

time: 36.7 us -> 36.2 us (0.986)
  waiting for transfers between devices: 1.35 us -> 0.87 us
    ppermute x1, waiting for transfers between devices: 1.35 us -> 0.87 us  [body(): other = lax.ppermute(near, 'rows', [(d, d ^ 1) for d in range(ndev)])]
    pallas_call x1 -> x2, Pallas kernels: 0.69 us -> 0.84 us  [the longest x1 0.46 us: prepare(): pl.pallas_call(points_kernel, out_shape=jax.ShapeDtypeStruct((rows, 256),...]
  transfers between devices with their start and end apart: 1 -> 1, of which waited for: 1 -> 1; matrix products, arithmetic and copies ran while one was open for 0% -> 0% of each run, Pallas kernels for 0% -> 1%
where the time goes in v5:
time: 36.2 us; the launch traced here: 36 us
  Pallas kernels  16.9 us (47%)
  blocking collectives  15.9 us (44%)
  local copies, waits for them, and re-layouts  1.63 us (5%)
  waiting for transfers between devices  0.87 us (2%)
  between operations  0.67 us (2%)
    all_to_all x1, blocking collectives, body(): lax.all_to_all(buffer, 'rows', 0, 0, axis_index_groups=cores, tiled=True)  15.9 us
    pallas_call x1, Pallas kernels, factorize(): pl.pallas_call(factor_kernel, out_shape=[jax.ShapeDtypeStruct((rows, widt...  15.8 us
    unnamed x4, local copies, waits for them, and re-layouts  1.63 us
    ppermute x1, waiting for transfers between devices, body(): other = lax.ppermute(near, 'rows', [(d, d ^ 1) for d in range(ndev)])  0.87 us
  transfers between devices with their start and end apart: 1, of which 1 were waited for; matrix products, arithmetic and copies ran while one was open for 0% of the time, Pallas kernels for 1%

profile of v5, /device:TPU:0, one launch (start us, length us, event | category | flops | bytes accessed | tf_op | source)
XLA Modules:
  0.0 36.0 jit_solution(4809274055881485070)
XLA Ops:
  0.6 0.0 copy-start.1
  0.6 0.7 %copy-done.1 = s32[2,256]{1,0:T(2,128)S(1)} copy-done((s32[2,256]{1,0:T(2,128)S(1)}, s32[2,256]{1,0:T(2,128)}, u32[]{:S(2)}) %copy-start.1) | copy-done | bytes 2072
  1.3 0.2 shard_map.42
  1.6 0.0 copy-start
  1.6 1.0 %copy-done = f32[64,1024]{1,0:T(8,128)S(1)} copy-done((f32[64,1024]{1,0:T(8,128)S(1)}, f32[64,1024]{1,0:T(8,128)}, u32[]{:S(2)}) %copy-start) | copy-done | bytes 262168
  2.5 0.4 %shard_map.43 = f32[16,16,128]{2,1,0:T(8,128)S(1)} custom-call(f32[64,1024]{1,0:T(8,128)S(1)} %copy-done, f32[32,128]{1,0:T(8,128)S(1)} %get-tuple-element.6.column_ref), custom_call_target="tpu_custom_call" | custom-call | tf_op jit(solution)/shard_map/pallas_call | solution.py:326
  2.9 15.9 %all_to_all.5 = f32[16,16,128]{2,1,0:T(8,128)S(1)} all-to-all(f32[16,16,128]{2,1,0:T(8,128)S(1)} %shard_map.43), channel_id=1, replica_groups={{0,2,4,6,8,10,12,14,16,18,20,22,24,26,28,30},{1,3,5,7,9,11,13,15,17,19,..., dimensions={0} | all-to-all | bytes 262144 | tf_op jit(solution)/shard_map/all_to_all | solution.py:372
  18.8 0.0 collective-permute-start
  18.8 0.5 %shard_map.41.points_ref = bf16[1024,256]{1,0:T(8,128)(2,1)S(1)} custom-call(f32[64,1024]{1,0:T(8,128)S(1)} %copy-done), custom_call_target="tpu_custom_call" | custom-call | flops 1310720 | bytes 786432 | tf_op jit(solution)/shard_map/pallas_call | solution.py:333
  19.3 0.9 %collective-permute-done.other_ref = f32[256,128]{1,0:T(8,128)S(1)} collective-permute-done((f32[256,128]{1,0:T(8,128)S(1)}, f32[256,128]{1,0:T(8,128)S(1)}, u32[]{:S(2)}, u32[]{:S(2)}) %collective-permute-start) | collective-permute-done | bytes 131104 | tf_op jit(solution)/shard_map/ppermute | solution.py:374
  20.2 15.8 %shard_map.44 = (bf16[1024,512]{1,0:T(8,128)(2,1)}, f32[1,1024]{1,0:T(1,128)}) custom-call(bf16[1024,256]{1,0:T(8,128)(2,1)S(1)} %shard_map.41.points_ref, f32[256,128]{1,0:T(8,128)S(1)} %bitcast.3, f32[256,128]{1,0:T(8,128)S(1)} %collective-permute-done.other_ref, f32[8,256]{1,0:T(8,128)S(1)} %get-tuple-element.7.target_ref), custom_call_target="tpu_custom_call" | custom-call | tf_op jit(solution)/shard_map/pallas_call | solution.py:348
Async XLA Ops:
  0.6 0.7 %copy-start.1 = (s32[2,256]{1,0:T(2,128)S(1)}, s32[2,256]{1,0:T(2,128)}, u32[]{:S(2)}) copy-start(s32[2,256]{1,0:T(2,128)} %pivots_ref.1) | copy-start | bytes 6148
  1.6 1.0 %copy-start = (f32[64,1024]{1,0:T(8,128)S(1)}, f32[64,1024]{1,0:T(8,128)}, u32[]{:S(2)}) copy-start(f32[64,1024]{1,0:T(8,128)} %points_ref.3) | copy-start | bytes 786436
  18.8 1.3 %collective-permute-start = (f32[256,128]{1,0:T(8,128)S(1)}, f32[256,128]{1,0:T(8,128)S(1)}, u32[]{:S(2)}, u32[]{:S(2)}) collective-permute-start(f32[256,128]{1,0:T(8,128)S(1)} %bitcast.2), channel_id=1, source_target_pairs={{0,1},{1,0},{2,3},{3,2},{4,5},{5,4},{6,7},{7,6},{8,9},{9,8},{10,11... | collective-permute-start | bytes 393224 | tf_op jit(solution)/shard_map/ppermute | solution.py:374

commit v6 on v5

--- a/solution.py
+++ b/solution.py
@@ -83,13 +83,20 @@
         inv[k] = lax.rsqrt(a)
         inv[k + 1] = (a * inv[k]) * root
         low[k + 1, k] = b * inv[k]
+        over = root * root
+        rest = {}
         for i in range(k + 2, STEP):
             low[i, k] = e[i, k] * inv[k]
-            low[i, k + 1] = (e[i, k + 1] - low[i, k] * low[k + 1, k]) * inv[k + 1]
+            rest[i] = e[i, k + 1] - low[i, k] * low[k + 1, k]
+            low[i, k + 1] = rest[i] * inv[k + 1]
         for m in range(k + 2, STEP):
             for i in range(m, STEP):
-                e[i, m] = (e[i, m] - low[i, k] * low[m, k]) - low[i, k + 1] * low[m, k + 1]
-    return low, inv
+                e[i, m] = e[i, m] - low[i, k] * low[m, k]
+                if i < k + 4:
+                    e[i, m] = e[i, m] - (rest[i] * (a * rest[m])) * over
+                else:
+                    e[i, m] = e[i, m] - low[i, k + 1] * low[m, k + 1]
+    return low, inv, a, over
 
 
 def panel_inverse(tiles, jobs, spread):
@@ -107,7 +114,7 @@
         for k in range(STEP):
             for i, row in spreader.rows(cols[k], k).items():
                 e[i, k] = row
-        low, inv = small_factor(e)
+        low, inv, pivot, over = small_factor(e)
         own = jnp.where(inside, jnp.where(lane - first == sub, 1.0, 0.0), tiles[s])
         upper = []
         own_rows = spreader.rows(own)
@@ -116,6 +123,7 @@
             for m in range(i):
                 acc = acc - low[i, m] * upper[m]
             upper.append(acc * inv[i])
+            last_row = acc
         done = upper[0]
         for i in range(1, STEP):
             done = jnp.where(sub == i, upper[i], done)
@@ -131,7 +139,10 @@
                     for m in range(k):
                         col = col - low[k, m] * mine[m]
                     mine.append(col * inv[k])
-                    acc = acc - mine[k] * upper[k]
+                    if k < STEP - 1:
+                        acc = acc - mine[k] * upper[k]
+                    else:
+                        acc = acc - (col * (pivot * last_row)) * over
             else:
                 if full is None:
                     full = [None] * STEP
@@ -150,7 +161,19 @@
     return jnp.concatenate(result, axis=0)
 
 
-def factor_kernel(points_ref, near_ref, other_ref, target_ref, factor_ref, diag_ref, work, squares, spread):
+def factor_kernel(
+    points_ref,
+    near_ref,
+    other_ref,
+    target_ref,
+    factor_hbm,
+    diag_ref,
+    work,
+    squares,
+    spread,
+    factor_ref,
+    sems,
+):
     rows, width = factor_ref.shape
     dim = near_ref.shape[1] // 2
     piv = width // 2
@@ -162,6 +185,7 @@
     place = lax.broadcasted_iota(jnp.int32, (PANEL, received.shape[0]), 1).astype(jnp.float32)
     piv_left = []
     piv_right = []
+    copies = []
 
     def kernel_block(block):
         def job():
@@ -212,6 +236,14 @@
             here = slice(first, first + CHUNK)
             factor_ref[here, start : start + PANEL] = new.astype(jnp.bfloat16)
             squares[here, :] = new * new if start == 0 else squares[here, :] + new * new
+            if first + CHUNK == rows:
+                cols = slice(start, start + PANEL)
+                copies.append(
+                    pltpu.make_async_copy(
+                        factor_ref.at[:, cols], factor_hbm.at[:, cols], sems.at[start // PANEL]
+                    )
+                )
+                copies[-1].start()
             if rights:
                 work[at, start + PANEL :] = work[at, start + PANEL :] - nt_dot(
                     left_form(new), jnp.concatenate(rights, axis=0)
@@ -252,6 +284,8 @@
         here = slice(first, first + LANES)
         sums = nn_dot(jnp.concatenate(thirds(squares[here, :]), axis=1), ones)
         diag_ref[:, here] = 1.0 - jnp.sum(jnp.where(keep, sums, 0.0), axis=0, keepdims=True)
+    for copy in copies:
+        copy.wait()
 
 
 def slots_kernel(ndev, rows, slots, pivots_ref, target_ref, column_ref):
@@ -352,11 +386,13 @@
             jax.ShapeDtypeStruct((1, rows), jnp.float32),
         ],
         in_specs=[VMEM] * 4,
-        out_specs=[VMEM] * 2,
+        out_specs=[pl.BlockSpec(memory_space=pl.ANY), VMEM],
         scratch_shapes=[
             pltpu.VMEM((width + rows, width), jnp.float32),
             pltpu.VMEM((rows, PANEL), jnp.float32),
             pltpu.VMEM(((STEP + 1) * PANEL, LANES), jnp.float32),
+            pltpu.VMEM((rows, width), jnp.bfloat16),
+            pltpu.SemaphoreType.DMA((width // PANEL,)),
         ],
         compiler_params=pltpu.CompilerParams(vmem_limit_bytes=48 * 2**20),
     )(points, near, other, target)

time: 36.2 us -> 36.5 us (level)
  no operation moved by 1% of the time
where the time goes in v6:
time: 36.5 us; the launch traced here: 36.3 us
  Pallas kernels  17.2 us (47%)
  blocking collectives  15.9 us (44%)
  local copies, waits for them, and re-layouts  1.63 us (4%)
  waiting for transfers between devices  0.87 us (2%)
  between operations  0.67 us (2%)
    pallas_call x1, Pallas kernels, factorize(): pl.pallas_call(factor_kernel, out_shape=[jax.ShapeDtypeStruct((rows, widt...  16.1 us
    all_to_all x1, blocking collectives, body(): lax.all_to_all(buffer, 'rows', 0, 0, axis_index_groups=cores, tiled=True)  15.9 us
    unnamed x4, local copies, waits for them, and re-layouts  1.63 us
    ppermute x1, waiting for transfers between devices, body(): other = lax.ppermute(near, 'rows', [(d, d ^ 1) for d in range(ndev)])  0.87 us
  transfers between devices with their start and end apart: 1, of which 1 were waited for; matrix products, arithmetic and copies ran while one was open for 0% of the time, Pallas kernels for 1%

profile of v6, /device:TPU:0, one launch (start us, length us, event | category | flops | bytes accessed | tf_op | source)
XLA Modules:
  0.0 36.3 jit_solution(8632888434825616036)
XLA Ops:
  0.6 0.0 copy-start.1
  0.6 0.7 %copy-done.1 = s32[2,256]{1,0:T(2,128)S(1)} copy-done((s32[2,256]{1,0:T(2,128)S(1)}, s32[2,256]{1,0:T(2,128)}, u32[]{:S(2)}) %copy-start.1) | copy-done | bytes 2072
  1.3 0.2 shard_map.42
  1.6 0.0 copy-start
  1.6 1.0 %copy-done = f32[64,1024]{1,0:T(8,128)S(1)} copy-done((f32[64,1024]{1,0:T(8,128)S(1)}, f32[64,1024]{1,0:T(8,128)}, u32[]{:S(2)}) %copy-start) | copy-done | bytes 262168
  2.5 0.4 %shard_map.43 = f32[16,16,128]{2,1,0:T(8,128)S(1)} custom-call(f32[64,1024]{1,0:T(8,128)S(1)} %copy-done, f32[32,128]{1,0:T(8,128)S(1)} %get-tuple-element.6.column_ref), custom_call_target="tpu_custom_call" | custom-call | tf_op jit(solution)/shard_map/pallas_call | solution.py:360
  2.9 15.9 %all_to_all.5 = f32[16,16,128]{2,1,0:T(8,128)S(1)} all-to-all(f32[16,16,128]{2,1,0:T(8,128)S(1)} %shard_map.43), channel_id=1, replica_groups={{0,2,4,6,8,10,12,14,16,18,20,22,24,26,28,30},{1,3,5,7,9,11,13,15,17,19,..., dimensions={0} | all-to-all | bytes 262144 | tf_op jit(solution)/shard_map/all_to_all | solution.py:408
  18.8 0.0 collective-permute-start
  18.8 0.5 %shard_map.41.points_ref = bf16[1024,256]{1,0:T(8,128)(2,1)S(1)} custom-call(f32[64,1024]{1,0:T(8,128)S(1)} %copy-done), custom_call_target="tpu_custom_call" | custom-call | flops 1310720 | bytes 786432 | tf_op jit(solution)/shard_map/pallas_call | solution.py:367
  19.3 0.9 %collective-permute-done.other_ref = f32[256,128]{1,0:T(8,128)S(1)} collective-permute-done((f32[256,128]{1,0:T(8,128)S(1)}, f32[256,128]{1,0:T(8,128)S(1)}, u32[]{:S(2)}, u32[]{:S(2)}) %collective-permute-start) | collective-permute-done | bytes 131104 | tf_op jit(solution)/shard_map/ppermute | solution.py:410
  20.2 16.1 %shard_map.44 = (bf16[1024,512]{1,0:T(8,128)(2,1)}, f32[1,1024]{1,0:T(1,128)}) custom-call(bf16[1024,256]{1,0:T(8,128)(2,1)S(1)} %shard_map.41.points_ref, f32[256,128]{1,0:T(8,128)S(1)} %bitcast.3, f32[256,128]{1,0:T(8,128)S(1)} %collective-permute-done.other_ref, f32[8,256]{1,0:T(8,128)S(1)} %get-tuple-element.7.target_ref), custom_call_target="tpu_custom_call" | custom-call | tf_op jit(solution)/shard_map/pallas_call | solution.py:382
Async XLA Ops:
  0.6 0.7 %copy-start.1 = (s32[2,256]{1,0:T(2,128)S(1)}, s32[2,256]{1,0:T(2,128)}, u32[]{:S(2)}) copy-start(s32[2,256]{1,0:T(2,128)} %pivots_ref.1) | copy-start | bytes 6148
  1.6 1.0 %copy-start = (f32[64,1024]{1,0:T(8,128)S(1)}, f32[64,1024]{1,0:T(8,128)}, u32[]{:S(2)}) copy-start(f32[64,1024]{1,0:T(8,128)} %points_ref.3) | copy-start | bytes 786436
  18.8 1.3 %collective-permute-start = (f32[256,128]{1,0:T(8,128)S(1)}, f32[256,128]{1,0:T(8,128)S(1)}, u32[]{:S(2)}, u32[]{:S(2)}) collective-permute-start(f32[256,128]{1,0:T(8,128)S(1)} %bitcast.2), channel_id=1, source_target_pairs={{0,1},{1,0},{2,3},{3,2},{4,5},{5,4},{6,7},{7,6},{8,9},{9,8},{10,11... | collective-permute-start | bytes 393224 | tf_op jit(solution)/shard_map/ppermute | solution.py:410

commit v7 on v5

--- a/solution.py
+++ b/solution.py
@@ -10,7 +10,7 @@
 PANEL = 128
 STEP = 8
 LANES = 128
-CHUNK = 128
+CHUNK = 512
 
 
 def halves(x):
@@ -248,10 +248,10 @@
     keep = lax.broadcasted_iota(jnp.int32, (LANES, LANES), 0) == lax.broadcasted_iota(
         jnp.int32, (LANES, LANES), 1
     )
+    sums = nn_dot(jnp.concatenate(thirds(squares[...]), axis=1), ones)
     for first in range(0, rows, LANES):
         here = slice(first, first + LANES)
-        sums = nn_dot(jnp.concatenate(thirds(squares[here, :]), axis=1), ones)
-        diag_ref[:, here] = 1.0 - jnp.sum(jnp.where(keep, sums, 0.0), axis=0, keepdims=True)
+        diag_ref[:, here] = 1.0 - jnp.sum(jnp.where(keep, sums[here], 0.0), axis=0, keepdims=True)
 
 
 def slots_kernel(ndev, rows, slots, pivots_ref, target_ref, column_ref):

time: 36.2 us -> 36 us (level)
  no operation moved by 1% of the time
where the time goes in v7:
time: 36 us; the launch traced here: 35.8 us
  Pallas kernels  16.7 us (46%)
  blocking collectives  15.9 us (44%)
  local copies, waits for them, and re-layouts  1.63 us (5%)
  waiting for transfers between devices  0.87 us (2%)
  between operations  0.67 us (2%)
    all_to_all x1, blocking collectives, body(): lax.all_to_all(buffer, 'rows', 0, 0, axis_index_groups=cores, tiled=True)  15.9 us
    pallas_call x1, Pallas kernels, factorize(): pl.pallas_call(factor_kernel, out_shape=[jax.ShapeDtypeStruct((rows, widt...  15.6 us
    unnamed x4, local copies, waits for them, and re-layouts  1.63 us
    ppermute x1, waiting for transfers between devices, body(): other = lax.ppermute(near, 'rows', [(d, d ^ 1) for d in range(ndev)])  0.87 us
  transfers between devices with their start and end apart: 1, of which 1 were waited for; matrix products, arithmetic and copies ran while one was open for 0% of the time, Pallas kernels for 1%

profile of v7, /device:TPU:0, one launch (start us, length us, event | category | flops | bytes accessed | tf_op | source)
XLA Modules:
  0.0 35.8 jit_solution(6259787838265960497)
XLA Ops:
  0.6 0.0 copy-start.1
  0.6 0.7 %copy-done.1 = s32[2,256]{1,0:T(2,128)S(1)} copy-done((s32[2,256]{1,0:T(2,128)S(1)}, s32[2,256]{1,0:T(2,128)}, u32[]{:S(2)}) %copy-start.1) | copy-done | bytes 2072
  1.3 0.2 shard_map.42
  1.6 0.0 copy-start
  1.6 1.0 %copy-done = f32[64,1024]{1,0:T(8,128)S(1)} copy-done((f32[64,1024]{1,0:T(8,128)S(1)}, f32[64,1024]{1,0:T(8,128)}, u32[]{:S(2)}) %copy-start) | copy-done | bytes 262168
  2.5 0.4 %shard_map.43 = f32[16,16,128]{2,1,0:T(8,128)S(1)} custom-call(f32[64,1024]{1,0:T(8,128)S(1)} %copy-done, f32[32,128]{1,0:T(8,128)S(1)} %get-tuple-element.6.column_ref), custom_call_target="tpu_custom_call" | custom-call | tf_op jit(solution)/shard_map/pallas_call | solution.py:326
  2.9 15.9 %all_to_all.5 = f32[16,16,128]{2,1,0:T(8,128)S(1)} all-to-all(f32[16,16,128]{2,1,0:T(8,128)S(1)} %shard_map.43), channel_id=1, replica_groups={{0,2,4,6,8,10,12,14,16,18,20,22,24,26,28,30},{1,3,5,7,9,11,13,15,17,19,..., dimensions={0} | all-to-all | bytes 262144 | tf_op jit(solution)/shard_map/all_to_all | solution.py:372
  18.8 0.0 collective-permute-start
  18.8 0.5 %shard_map.41.points_ref = bf16[1024,256]{1,0:T(8,128)(2,1)S(1)} custom-call(f32[64,1024]{1,0:T(8,128)S(1)} %copy-done), custom_call_target="tpu_custom_call" | custom-call | flops 1310720 | bytes 786432 | tf_op jit(solution)/shard_map/pallas_call | solution.py:333
  19.3 0.9 %collective-permute-done.other_ref = f32[256,128]{1,0:T(8,128)S(1)} collective-permute-done((f32[256,128]{1,0:T(8,128)S(1)}, f32[256,128]{1,0:T(8,128)S(1)}, u32[]{:S(2)}, u32[]{:S(2)}) %collective-permute-start) | collective-permute-done | bytes 131104 | tf_op jit(solution)/shard_map/ppermute | solution.py:374
  20.2 15.6 %shard_map.44 = (bf16[1024,512]{1,0:T(8,128)(2,1)}, f32[1,1024]{1,0:T(1,128)}) custom-call(bf16[1024,256]{1,0:T(8,128)(2,1)S(1)} %shard_map.41.points_ref, f32[256,128]{1,0:T(8,128)S(1)} %bitcast.3, f32[256,128]{1,0:T(8,128)S(1)} %collective-permute-done.other_ref, f32[8,256]{1,0:T(8,128)S(1)} %get-tuple-element.7.target_ref), custom_call_target="tpu_custom_call" | custom-call | tf_op jit(solution)/shard_map/pallas_call | solution.py:348
Async XLA Ops:
  0.6 0.7 %copy-start.1 = (s32[2,256]{1,0:T(2,128)S(1)}, s32[2,256]{1,0:T(2,128)}, u32[]{:S(2)}) copy-start(s32[2,256]{1,0:T(2,128)} %pivots_ref.1) | copy-start | bytes 6148
  1.6 1.0 %copy-start = (f32[64,1024]{1,0:T(8,128)S(1)}, f32[64,1024]{1,0:T(8,128)}, u32[]{:S(2)}) copy-start(f32[64,1024]{1,0:T(8,128)} %points_ref.3) | copy-start | bytes 786436
  18.8 1.3 %collective-permute-start = (f32[256,128]{1,0:T(8,128)S(1)}, f32[256,128]{1,0:T(8,128)S(1)}, u32[]{:S(2)}, u32[]{:S(2)}) collective-permute-start(f32[256,128]{1,0:T(8,128)S(1)} %bitcast.2), channel_id=1, source_target_pairs={{0,1},{1,0},{2,3},{3,2},{4,5},{5,4},{6,7},{7,6},{8,9},{9,8},{10,11... | collective-permute-start | bytes 393224 | tf_op jit(solution)/shard_map/ppermute | solution.py:374

commit v8 on v7

--- a/solution.py
+++ b/solution.py
@@ -10,7 +10,7 @@
 PANEL = 128
 STEP = 8
 LANES = 128
-CHUNK = 512
+CHUNK = 1024
 
 
 def halves(x):
@@ -186,8 +186,8 @@
         def job():
             right = jnp.concatenate(piv_right[2 * pair : 2 * pair + 2], axis=0)
             cols = slice(2 * pair * PANEL, 2 * (pair + 1) * PANEL)
-            here = slice(first, first + 2 * CHUNK)
-            work[width + first : width + first + 2 * CHUNK, cols] = jnp.exp(
+            here = slice(first, first + CHUNK)
+            work[width + first : width + first + CHUNK, cols] = jnp.exp(
                 nt_dot(points_ref[here, :], right)
             )
 
@@ -223,7 +223,7 @@
     jobs += [
         kernel_rows(first, pair)
         for pair in range(width // PANEL // 2)
-        for first in range(0, rows, 2 * CHUNK)
+        for first in range(0, rows, CHUNK)
     ]
     for start in range(0, width, PANEL):
         block = slice(start, start + PANEL)

time: 36 us -> 35.9 us (level)
  no operation moved by 1% of the time
where the time goes in v8:
time: 35.9 us; the launch traced here: 35.6 us
  Pallas kernels  16.6 us (46%)
  blocking collectives  15.9 us (44%)
  local copies, waits for them, and re-layouts  1.63 us (5%)
  waiting for transfers between devices  0.87 us (2%)
  between operations  0.67 us (2%)
    all_to_all x1, blocking collectives, body(): lax.all_to_all(buffer, 'rows', 0, 0, axis_index_groups=cores, tiled=True)  15.9 us
    pallas_call x1, Pallas kernels, factorize(): pl.pallas_call(factor_kernel, out_shape=[jax.ShapeDtypeStruct((rows, widt...  15.5 us
    unnamed x4, local copies, waits for them, and re-layouts  1.63 us
    ppermute x1, waiting for transfers between devices, body(): other = lax.ppermute(near, 'rows', [(d, d ^ 1) for d in range(ndev)])  0.87 us
  transfers between devices with their start and end apart: 1, of which 1 were waited for; matrix products, arithmetic and copies ran while one was open for 0% of the time, Pallas kernels for 1%

profile of v8, /device:TPU:0, one launch (start us, length us, event | category | flops | bytes accessed | tf_op | source)
XLA Modules:
  0.0 35.6 jit_solution(425943520190399788)
XLA Ops:
  0.6 0.0 copy-start.1
  0.6 0.7 %copy-done.1 = s32[2,256]{1,0:T(2,128)S(1)} copy-done((s32[2,256]{1,0:T(2,128)S(1)}, s32[2,256]{1,0:T(2,128)}, u32[]{:S(2)}) %copy-start.1) | copy-done | bytes 2072
  1.3 0.2 shard_map.42
  1.6 0.0 copy-start
  1.6 1.0 %copy-done = f32[64,1024]{1,0:T(8,128)S(1)} copy-done((f32[64,1024]{1,0:T(8,128)S(1)}, f32[64,1024]{1,0:T(8,128)}, u32[]{:S(2)}) %copy-start) | copy-done | bytes 262168
  2.5 0.4 %shard_map.43 = f32[16,16,128]{2,1,0:T(8,128)S(1)} custom-call(f32[64,1024]{1,0:T(8,128)S(1)} %copy-done, f32[32,128]{1,0:T(8,128)S(1)} %get-tuple-element.6.column_ref), custom_call_target="tpu_custom_call" | custom-call | tf_op jit(solution)/shard_map/pallas_call | solution.py:326
  2.9 15.9 %all_to_all.5 = f32[16,16,128]{2,1,0:T(8,128)S(1)} all-to-all(f32[16,16,128]{2,1,0:T(8,128)S(1)} %shard_map.43), channel_id=1, replica_groups={{0,2,4,6,8,10,12,14,16,18,20,22,24,26,28,30},{1,3,5,7,9,11,13,15,17,19,..., dimensions={0} | all-to-all | bytes 262144 | tf_op jit(solution)/shard_map/all_to_all | solution.py:372
  18.8 0.0 collective-permute-start
  18.8 0.5 %shard_map.41.points_ref = bf16[1024,256]{1,0:T(8,128)(2,1)S(1)} custom-call(f32[64,1024]{1,0:T(8,128)S(1)} %copy-done), custom_call_target="tpu_custom_call" | custom-call | flops 1310720 | bytes 786432 | tf_op jit(solution)/shard_map/pallas_call | solution.py:333
  19.3 0.9 %collective-permute-done.other_ref = f32[256,128]{1,0:T(8,128)S(1)} collective-permute-done((f32[256,128]{1,0:T(8,128)S(1)}, f32[256,128]{1,0:T(8,128)S(1)}, u32[]{:S(2)}, u32[]{:S(2)}) %collective-permute-start) | collective-permute-done | bytes 131104 | tf_op jit(solution)/shard_map/ppermute | solution.py:374
  20.2 15.5 %shard_map.44 = (bf16[1024,512]{1,0:T(8,128)(2,1)}, f32[1,1024]{1,0:T(1,128)}) custom-call(bf16[1024,256]{1,0:T(8,128)(2,1)S(1)} %shard_map.41.points_ref, f32[256,128]{1,0:T(8,128)S(1)} %bitcast.3, f32[256,128]{1,0:T(8,128)S(1)} %collective-permute-done.other_ref, f32[8,256]{1,0:T(8,128)S(1)} %get-tuple-element.7.target_ref), custom_call_target="tpu_custom_call" | custom-call | tf_op jit(solution)/shard_map/pallas_call | solution.py:348
Async XLA Ops:
  0.6 0.7 %copy-start.1 = (s32[2,256]{1,0:T(2,128)S(1)}, s32[2,256]{1,0:T(2,128)}, u32[]{:S(2)}) copy-start(s32[2,256]{1,0:T(2,128)} %pivots_ref.1) | copy-start | bytes 6148
  1.6 1.0 %copy-start = (f32[64,1024]{1,0:T(8,128)S(1)}, f32[64,1024]{1,0:T(8,128)}, u32[]{:S(2)}) copy-start(f32[64,1024]{1,0:T(8,128)} %points_ref.3) | copy-start | bytes 786436
  18.8 1.3 %collective-permute-start = (f32[256,128]{1,0:T(8,128)S(1)}, f32[256,128]{1,0:T(8,128)S(1)}, u32[]{:S(2)}, u32[]{:S(2)}) collective-permute-start(f32[256,128]{1,0:T(8,128)S(1)} %bitcast.2), channel_id=1, source_target_pairs={{0,1},{1,0},{2,3},{3,2},{4,5},{5,4},{6,7},{7,6},{8,9},{9,8},{10,11... | collective-permute-start | bytes 393224 | tf_op jit(solution)/shard_map/ppermute | solution.py:374
